TPU v7x, 128 devices: a whole 4x4x4 slice. The times are simulated.
128 devices in a mesh: panel: 16 (over x, z_lo, core), rep: 8 (over y, z_hi).
Axes of the slice: x: 4, y: 4, z: 4 (z_hi: 2, z_lo: 2; z = z_hi * 2 + z_lo), core: 2. Of those that a mesh axis runs over, the one named last changes fastest.
Arguments:
- activations: float32 [393216, 1024], P(('panel', 'rep')), may hold values from 0 to 48
- out_grads: float32 [393216, 256], P(('panel', 'rep')), may hold values from -8 to 8
- factor_a: float32 [1024, 1024], P('panel'), may hold values from -7 to 27
- factor_g: float32 [256, 256], P('panel'), may hold values from -7 to 27
- inverse_a: float32 [1024, 1024], P('panel'), may hold values from -0.1875 to 0.1875
- inverse_g: float32 [256, 256], P('panel'), may hold values from -0.375 to 0.375
Outputs:
- new_factor_a: float32 [1024, 1024], P('panel')
- new_factor_g: float32 [256, 256], P('panel')
- precond_grad: float32 [1024, 256], P('panel')
All inputs are finite; a program needn't handle non-finite values.
Results may differ from a plain program's by a relative error of at most 0.000076.
Values sent between devices are 32-bit elements; how exact they have to be, the bound alone decides.
No kernel may reach another device: no remote copies, remote signals or barrier semaphores. Data moves between devices by JAX's collectives and lax.ppermute only.
A program may use at most 128 MiB of HBM per device.

v0:
```python
import jax
import jax.numpy as jnp
from jax import lax
from jax.sharding import PartitionSpec as P

decay_rate = 0.6


def gram_rows(left, right):
    return lax.dot_general(
        left,
        right,
        (((0,), (0,)), ((), ())),
        precision=lax.Precision.HIGHEST,
        preferred_element_type=jnp.float32,
    )


def local(activations, out_grads, factor_a, factor_g, inverse_a, inverse_g):
    total_rows = activations.shape[0] * lax.axis_size("panel") * lax.axis_size("rep")
    cin = activations.shape[1]
    panel_a = factor_a.shape[0]
    panel_g = factor_g.shape[0]
    joint_all, small_all = lax.psum(
        (
            jnp.concatenate(
                [gram_rows(activations, activations), gram_rows(activations, out_grads)], axis=1
            ),
            gram_rows(out_grads, out_grads),
        ),
        ("panel", "rep"),
    )
    owner = lax.axis_index("panel")
    joint = lax.dynamic_slice_in_dim(joint_all, owner * panel_a, panel_a, 0)
    small = lax.dynamic_slice_in_dim(small_all, owner * panel_g, panel_g, 0)
    new_factor_a = decay_rate * factor_a + (1.0 - decay_rate) * (joint[:, :cin] / total_rows)
    new_factor_g = decay_rate * factor_g + (1.0 - decay_rate) * small
    grad_rows = joint[:, cin:]
    inverse_full = lax.all_gather(inverse_g, "panel", axis=0, tiled=True)
    right = jnp.dot(
        grad_rows, inverse_full, precision=lax.Precision.HIGHEST, preferred_element_type=jnp.float32
    )
    precond_grad = jnp.dot(
        inverse_a,
        lax.all_gather(right, "panel", axis=0, tiled=True),
        precision=lax.Precision.HIGHEST,
        preferred_element_type=jnp.float32,
    )
    return (new_factor_a, new_factor_g, precond_grad)


def solution(mesh):
    in_specs = (
        P(("panel", "rep"), None),
        P(("panel", "rep"), None),
        P("panel", None),
        P("panel", None),
        P("panel", None),
        P("panel", None),
    )
    out_specs = (P("panel", None), P("panel", None), P("panel", None))
    return jax.shard_map(local, mesh=mesh, in_specs=in_specs, out_specs=out_specs, check_vma=False)
```

profile of v0, /device:TPU:1, one launch (start us, length us, event | category | flops | bytes accessed | tf_op | source)
XLA Modules:
  0.0 276.4 jit_solution(9895914609218290272)
XLA Ops:
  7.2 0.0 copy-start
  7.2 0.0 all-reduce.3.cloned.1.call-start
  7.2 0.0 copy-start.1
  7.2 45.6 %fusion.3 = f32[1024,1024]{0,1:T(8,128)S(1)} fusion(f32[3072,1024]{1,0:T(8,128)} %param.6), kind=kOutput, calls=%fused_computation.7 | convolution fusion | flops 38654705664 | bytes 16777216 | tf_op jit(solution)/shard_map/dot_general | solution.py:10
  52.9 0.0 copy-done
  52.9 0.0 copy-done.1
  52.9 11.1 %fusion.4 = f32[1024,256]{0,1:T(8,128)S(1)} fusion(f32[3072,1024]{1,0:T(8,128)S(1)} %copy-done.1, f32[3072,256]{1,0:T(8,128)S(1)} %copy-done), kind=kOutput, calls=%fused_computation.8 | convolution fusion | flops 9663676416 | bytes 16777216 | tf_op jit(solution)/shard_map/dot_general | solution.py:10
  64.0 6.1 %fusion.5 = f32[256,256]{1,0:T(8,128)} fusion(f32[3072,256]{1,0:T(8,128)S(1)} %copy-done), kind=kOutput, calls=%fused_computation.9 | convolution fusion | flops 2415919104 | bytes 3407872 | tf_op jit(solution)/shard_map/dot_general | solution.py:10
  70.0 3.2 %pad_maximum_fusion = f32[1024,1280]{0,1:T(8,128)} fusion(f32[1024,256]{0,1:T(8,128)S(1)} %fusion.4, f32[1024,1024]{0,1:T(8,128)S(1)} %fusion.3), kind=kLoop, calls=%fused_computation | loop fusion | flops 1310720 | bytes 10485760 | tf_op jit(solution)/shard_map/concatenate | solution.py:26
  73.2 0.0 copy-start.2
  73.2 0.0 all-reduce.3.cloned.1.call-update
  73.3 0.0 all-gather.2.cloned.1.call-start
  73.3 0.6 copy-done.2
  74.0 22.2 %all_gather.6 = f32[256,256]{1,0:T(8,128)S(1)} all-gather(f32[16,256]{1,0:T(8,128)S(1)} %copy-done.2), channel_id=1, replica_groups=mesh['panel'=16,'rep'=8] {'panel'}, dimensions={0}, use_global_device_ids=true | all-gather | bytes 278528 | tf_op jit(solution)/shard_map/all_gather | solution.py:39
  96.1 137.2 %all-reduce.3.cloned.1.call-done = (f32[1024,1280]{0,1:T(8,128)}, f32[256,256]{1,0:T(8,128)}) async-done(((f32[1024,1280]{0,1:T(8,128)}, f32[256,256]{1,0:T(8,128)}), (f32[1024,1280]{0,1:T(8,128)}, f32[256,256]{1,0:T(8,128)})) %all-reduce.3.cloned.1.call-update) | async-done | bytes 5505040 | tf_op jit(solution)/shard_map/psum | solution.py:24
  233.4 2.0 fusion.1
  235.3 0.0 all-gather.2.cloned.1.call-update
  235.4 2.0 copy.9
  237.3 2.2 fusion
  239.6 1.9 copy.10
  241.5 0.0 copy-done.3
  241.5 1.3 multiply_add_fusion
  242.8 24.1 %all-gather.2.cloned.1.call-done = f32[1024,256]{1,0:T(8,128)} async-done(((f32[64,256]{1,0:T(8,128)}), f32[1024,256]{1,0:T(8,128)}) %all-gather.2.cloned.1.call-update) | async-done | bytes 1048592 | tf_op jit(solution)/shard_map/all_gather | solution.py:45
  267.0 2.6 convolution_bitcast_fusion
  (1 shorter events, 0.0 us)
Async XLA Ops:
  7.2 45.7 %copy-start = (f32[3072,256]{1,0:T(8,128)S(1)}, f32[3072,256]{1,0:T(8,128)}, u32[]{:S(2)}) copy-start(f32[3072,256]{1,0:T(8,128)} %param.7) | copy-start | bytes 9437188
  7.2 226.2 %all-reduce.3.cloned.1.call-start = ((), (), s32[]{:S(2)}) async-start(), calls=%async_computation.1 | async-start | bytes 11010048 | tf_op jit(solution)/shard_map/psum | solution.py:24
  7.2 45.7 %copy-start.1 = (f32[3072,1024]{1,0:T(8,128)S(1)}, f32[3072,1024]{1,0:T(8,128)}, u32[]{:S(2)}) copy-start(f32[3072,1024]{1,0:T(8,128)} %param.6) | copy-start | bytes 37748740
  73.2 0.7 copy-start.2
  73.2 168.3 %copy-start.3 = (f32[16,256]{1,0:T(8,128)S(1)}, f32[16,256]{1,0:T(8,128)}, u32[]{:S(2)}) copy-start(f32[16,256]{1,0:T(8,128)} %param.9) | copy-start | bytes 49156
  73.3 193.7 %all-gather.2.cloned.1.call-start = ((), (), s32[]{:S(2)}) async-start(), calls=%async_computation | async-start | bytes 1114112 | tf_op jit(solution)/shard_map/all_gather | solution.py:45
Sparse Core Ops, SparseCore 0:
  73.4 159.9 all-reduce.2
  235.6 31.2 all-gather.1
where the time goes:
time: 277 us; the launch traced here: 276 us
  waiting for transfers between devices  161 us (58%)
  matrix products  67.4 us (24%)
  blocking collectives  22.2 us (8%)
  between operations  14.1 us (5%)
  other arithmetic  6.75 us (2%)
  local copies, waits for them, and re-layouts  4.56 us (2%)
    psum x1, waiting for transfers between devices, local(): lax.psum((jnp.concatenate([gram_rows(activations, activations), gram_rows...  137 us
    dot_general x3, matrix products, gram_rows(): lax.dot_general(left, right, (((0,), (0,)), ((), ())), precision=lax.Prec...  62.8 us
    all_gather x1, waiting for transfers between devices, local(): lax.all_gather(right, 'panel', axis=0, tiled=True)  24.1 us
    all_gather x1, blocking collectives, local(): inverse_full = lax.all_gather(inverse_g, 'panel', axis=0, tiled=True)  22.2 us
  transfers between devices with their start and end apart: 2, of which 2 were waited for; matrix products, arithmetic and copies ran while one was open for 3% of the time, Pallas kernels for 0%

commit v1 on v0

v1 whole, which is shorter than its diff:
```python
import functools

import jax
import jax.numpy as jnp
from jax import lax
from jax.experimental import pallas as pl
from jax.experimental.pallas import tpu as pltpu
from jax.sharding import PartitionSpec as P

decay_rate = 0.6
F32 = jnp.float32
BF16 = jnp.bfloat16
SUB = ("x", "zl", "co", "y", "zh")
SIZES = (4, 2, 2, 4, 2)
CHIPS = ("x", "zl", "y", "zh")
VMEM = 58 * 2**20


def split(block):
    high = block.astype(BF16)
    return high, (block - high.astype(F32)).astype(BF16)


def gram(left, right):
    return lax.dot_general(left, right, (((0,), (0,)), ((), ())), preferred_element_type=F32)


def gram3(lh, ll, rh, rl):
    return gram(lh, rh) + gram(lh, rl) + gram(ll, rh)


def grad_kernel(core_ref, a_ref, g_ref, mine_ref, other_ref, grad, small):
    step = pl.program_id(0)
    gh, gl = split(g_ref[...])
    ah, al = split(a_ref[...])

    @pl.when(step == 0)
    def _():
        grad[...] = jnp.zeros_like(grad)
        small[...] = jnp.zeros_like(small)

    for j in range(0, grad.shape[0], 256):
        c = slice(j, j + 256)
        grad[c, :] += gram3(ah[:, c], al[:, c], gh, gl)
    small[...] += gram3(gh, gl, gh, gl)

    @pl.when(step == pl.num_programs(0) - 1)
    def _():
        core = core_ref[0]
        for which, out in ((core, mine_ref), (1 - core, other_ref)):
            for q in range(8):
                owner = 2 * q + which
                rows = pl.ds(pl.multiple_of(owner * 64, 64), 64)
                for half in range(2):
                    cols = slice(half * 128, half * 128 + 128)
                    tile = slice(half * 8, half * 8 + 8)
                    out[q * 8 : q * 8 + 8, tile, :] = grad[rows, cols].reshape(8, 8, 128)
                for y in range(4):
                    srows = pl.ds(pl.multiple_of(owner * 16 + 8 * (y // 2), 8), 8)
                    part = small[srows, 128 * (y % 2) : 128 * (y % 2) + 128]
                    out[q * 8 + 2 * y, 16:24, :] = part
                    out[q * 8 + 2 * y + 1, 16:24, :] = part


def grad_parts(core, activations, out_grads):
    rows, cin = activations.shape
    cout = out_grads.shape[1]
    tile = 512
    shape = jax.ShapeDtypeStruct((64, 24, 128), F32)
    spec = pl.BlockSpec((64, 24, 128), lambda k: (0, 0, 0))
    return pl.pallas_call(
        grad_kernel,
        grid=(rows // tile,),
        in_specs=[
            pl.BlockSpec(memory_space=pltpu.SMEM),
            pl.BlockSpec((tile, cin), lambda k: (k, 0)),
            pl.BlockSpec((tile, cout), lambda k: (k, 0)),
        ],
        out_specs=[spec, spec],
        out_shape=[shape, shape],
        scratch_shapes=[pltpu.VMEM((cin, cout), F32), pltpu.VMEM((cout, cout), F32)],
        compiler_params=pltpu.CompilerParams(vmem_limit_bytes=VMEM),
        cost_estimate=pl.CostEstimate(flops=6 * rows * (cin + cout) * cout, bytes_accessed=4 * rows * (cin + cout), transcendentals=0),
        name="grad_parts",
    )(core, activations, out_grads)


def stat_kernel(core_ref, a_ref, mine_ref, other_ref, acc):
    step = pl.program_id(0)
    cin = acc.shape[0]
    ah, al = split(a_ref[...])

    @pl.when(step == 0)
    def _():
        acc[...] = jnp.zeros_like(acc)

    for i in range(0, cin, 256):
        ci, cj = slice(i, i + 256), slice(i, cin)
        acc[ci, cj] += gram3(ah[:, ci], al[:, ci], ah[:, cj], al[:, cj])

    @pl.when(step == pl.num_programs(0) - 1)
    def _():
        for i in range(0, cin, 256):
            for j in range(i + 256, cin, 256):
                acc[j : j + 256, i : i + 256] = acc[i : i + 256, j : j + 256].T
        core = core_ref[0]
        for which, out in ((core, mine_ref), (1 - core, other_ref)):
            for q in range(8):
                rows = pl.ds(pl.multiple_of((2 * q + which) * 64, 64), 64)
                out[q * 64 : q * 64 + 64, :] = acc[rows, :]


def stat_parts(core, activations):
    rows, cin = activations.shape
    tile = 512
    shape = jax.ShapeDtypeStruct((cin // 2, cin), F32)
    spec = pl.BlockSpec((cin // 2, cin), lambda k: (0, 0))
    return pl.pallas_call(
        stat_kernel,
        grid=(rows // tile,),
        in_specs=[
            pl.BlockSpec(memory_space=pltpu.SMEM),
            pl.BlockSpec((tile, cin), lambda k: (k, 0)),
        ],
        out_specs=[spec, spec],
        out_shape=[shape, shape],
        scratch_shapes=[pltpu.VMEM((cin, cin), F32)],
        compiler_params=pltpu.CompilerParams(vmem_limit_bytes=VMEM),
        cost_estimate=pl.CostEstimate(flops=4 * rows * cin * cin, bytes_accessed=4 * rows * cin, transcendentals=0),
        name="stat_parts",
    )(core, activations)


def final_kernel(inv_a_ref, grad_ref, inv_g_ref, out_ref):
    halves = [grad_ref[:, 8 * h : 8 * h + 8, :].reshape(1024, 128) for h in range(2)]
    grad = jnp.concatenate(halves, axis=1)
    left = jnp.dot(inv_a_ref[...], grad, precision=lax.Precision.HIGHEST, preferred_element_type=F32)
    out_ref[...] = jnp.dot(left, inv_g_ref[...], precision=lax.Precision.HIGHEST, preferred_element_type=F32)


def final(inverse_a, grad, inverse_g):
    return pl.pallas_call(
        final_kernel,
        out_shape=jax.ShapeDtypeStruct((inverse_a.shape[0], 256), F32),
        compiler_params=pltpu.CompilerParams(vmem_limit_bytes=VMEM),
        name="final",
    )(inverse_a, grad, inverse_g)


def pairs(move):
    index = lambda c: (((c[0] * 2 + c[1]) * 2 + c[2]) * 4 + c[3]) * 2 + c[4]
    out = []
    for flat in range(128):
        zh, rest = flat % 2, flat // 2
        y, rest = rest % 4, rest // 4
        co, rest = rest % 2, rest // 2
        zl, x = rest % 2, rest // 2
        out.append((flat, index(move(x, zl, co, y, zh))))
    return out


CORE = pairs(lambda x, zl, co, y, zh: (x, zl, 1 - co, y, zh))
Z1 = pairs(lambda x, zl, co, y, zh: (x, 1 - zl, co, y, zh))
Z2 = pairs(lambda x, zl, co, y, zh: (x, 1 - zl, co, y, 1 - zh))
Y1 = pairs(lambda x, zl, co, y, zh: (x, zl, co, y ^ 1, zh))
Y2 = pairs(lambda x, zl, co, y, zh: (x, zl, co, 3 - y, zh))
X1 = pairs(lambda x, zl, co, y, zh: (x ^ 1, zl, co, y, zh))
X2 = pairs(lambda x, zl, co, y, zh: (3 - x, zl, co, y, zh))


def move(array, table):
    return lax.ppermute(array, SUB, table)


def join(array, table, axis, late):
    got = move(array, table)
    return jnp.concatenate([jnp.where(late, got, array), jnp.where(late, array, got)], axis=axis)


def local(activations, out_grads, factor_a, factor_g, inverse_a, inverse_g):
    total_rows = activations.shape[0] * 128
    x, zl, co, y, zh = (lax.axis_index(n) for n in SUB)
    core = co.astype(jnp.int32).reshape(1)

    padded = jnp.pad(inverse_g, ((0, 48), (0, 0)))
    inv_g = lax.all_gather(padded, ("x", "zl", "co"), axis=0, tiled=False)[:, :16].reshape(256, 256)

    g_mine, g_other = grad_parts(core, activations, out_grads)
    g_sum = g_mine + move(g_other, CORE)
    g_all = lax.all_to_all(g_sum, CHIPS, 0, 0, tiled=True)
    s_mine, s_other = stat_parts(core, activations)
    s_sum = s_mine + move(s_other, CORE)
    g_own = jnp.sum(g_all, axis=0)
    s_all = lax.all_to_all(s_sum.reshape(64, 8, 1024), CHIPS, 0, 0, tiled=True)

    block = g_own[:16].reshape(1, 1, 1, 1, 1, 16, 128)
    block = join(block, Z1, 1, zl == 1)
    block = join(block, Z2, 4, zh == 1)
    block = join(block, Y1, 3, y % 2 == 1)
    block = join(block, Y2, 3, y >= 2)
    block = join(block, X1, 0, x % 2 == 1)
    block = join(block, X2, 0, x >= 2)
    block = join(block, CORE, 2, co == 1)
    precond_grad = final(inverse_a, block.reshape(128, 16, 128), inv_g)

    s_own = jnp.concatenate([jnp.sum(s_all, axis=0), g_own[16:]], axis=1)
    spread = jnp.broadcast_to(s_own[None], (8,) + s_own.shape)
    rows = lax.all_to_all(spread, ("y", "zh"), 0, 0, tiled=True)
    stat_a = rows[:, :, :1024].reshape(64, 1024) / total_rows
    tiles = rows[::2, :, 1024:].reshape(2, 2, 8, 128)
    stat_g = tiles.transpose(0, 2, 1, 3).reshape(16, 256)
    new_factor_a = decay_rate * factor_a + (1.0 - decay_rate) * stat_a
    new_factor_g = decay_rate * factor_g + (1.0 - decay_rate) * stat_g
    return new_factor_a, new_factor_g, precond_grad


def solution(mesh):
    fine = jax.sharding.Mesh(mesh.devices.reshape(SIZES), SUB)
    rows = P(SUB, None)
    panel = P(("x", "zl", "co"), None)
    return jax.shard_map(
        local,
        mesh=fine,
        in_specs=(rows, rows, panel, panel, panel, panel),
        out_specs=(panel, panel, panel),
        check_vma=False,
    )
```

time: 277 us -> 150 us (0.54)
  waiting for transfers between devices: 161 us -> 31.1 us
  matrix products: 67.4 us -> 0 us
  Pallas kernels: 0 us -> 36.6 us
  starting transfers between devices: 0.08 us -> 31.2 us
  blocking collectives: 22.2 us -> 26.2 us
    psum x1 -> x0, waiting for transfers between devices: 137 us -> none  [local(): lax.psum((jnp.concatenate([gram_rows(activations, activations), gram_rows...]
    dot_general x5 -> x0, matrix products: 67.4 us -> none  [the longest x3 62.8 us: gram_rows(): lax.dot_general(left, right, (((0,), (0,)), ((), ())), precision=lax.Prec...]
    pallas_call x0 -> x3, Pallas kernels: none -> 36.6 us  [the longest x1 20.5 us: stat_parts(): pl.pallas_call(stat_kernel, grid=(rows // tile,), in_specs=[pl.BlockSpec(...]
    ppermute x0 -> x9, waiting for transfers between devices: none -> 26.8 us  [move(): return lax.ppermute(array, SUB, table)]
    all_to_all x0 -> x1, blocking collectives: none -> 26.2 us  [local(): g_all = lax.all_to_all(g_sum, CHIPS, 0, 0, tiled=True)]
    all_gather x1, waiting for transfers between devices: 24.1 us -> 0.01 us  [local(): lax.all_gather(padded, ('x', 'zl', 'co'), axis=0, tiled=False)[:, :16]]
    all_gather x1 -> x0, blocking collectives: 22.2 us -> none  [local(): inverse_full = lax.all_gather(inverse_g, 'panel', axis=0, tiled=True)]
    ppermute x0 -> x9, starting transfers between devices: none -> 20.7 us  [move(): return lax.ppermute(array, SUB, table)]
  transfers between devices with their start and end apart: 2 -> 12, of which waited for: 2 -> 6; matrix products, arithmetic and copies ran while one was open for 3% -> 6% of each run, Pallas kernels for 0% -> 16%
where the time goes in v1:
time: 150 us
  Pallas kernels  36.6 us (24%)
  starting transfers between devices  31.2 us (21%)
  waiting for transfers between devices  31.1 us (21%)
  blocking collectives  26.2 us (17%)
  between operations  14.2 us (9%)
  other arithmetic  7.21 us (5%)
  local copies, waits for them, and re-layouts  3.09 us (2%)
    ppermute x9, waiting for transfers between devices, move(): return lax.ppermute(array, SUB, table)  26.8 us
    all_to_all x1, blocking collectives, local(): g_all = lax.all_to_all(g_sum, CHIPS, 0, 0, tiled=True)  26.2 us
    ppermute x9, starting transfers between devices, move(): return lax.ppermute(array, SUB, table)  20.7 us
    pallas_call x1, Pallas kernels, stat_parts(): pl.pallas_call(stat_kernel, grid=(rows // tile,), in_specs=[pl.BlockSpec(...  20.5 us
    pallas_call x1, Pallas kernels, grad_parts(): pl.pallas_call(grad_kernel, grid=(rows // tile,), in_specs=[pl.BlockSpec(...  13 us
    all_to_all x1, starting transfers between devices, local(): rows = lax.all_to_all(spread, ('y', 'zh'), 0, 0, tiled=True)  5.44 us
    all_to_all x1, starting transfers between devices, local(): s_all = lax.all_to_all(s_sum.reshape(64, 8, 1024), CHIPS, 0, 0, tiled=True)  5.02 us
    all_to_all x1, waiting for transfers between devices, local(): rows = lax.all_to_all(spread, ('y', 'zh'), 0, 0, tiled=True)  4.27 us
  transfers between devices with their start and end apart: 12, of which 6 were waited for; matrix products, arithmetic and copies ran while one was open for 6% of the time, Pallas kernels for 16%

profile of v1, /device:TPU:1, one launch (start us, length us, event | category | flops | bytes accessed | tf_op | source)
XLA Modules:
  0.0 149.6 jit_solution(7829407796743522522)
XLA Ops:
  7.2 13.0 %grad_parts.1 = (f32[64,24,128]{2,1,0:T(8,128)}, f32[64,24,128]{2,1,0:T(8,128)}) custom-call(s32[1]{0:T(128)} %bitcast.core_ref, f32[3072,1024]{1,0:T(8,128)} %a_ref.3, f32[3072,256]{1,0:T(8,128)} %g_ref.1), custom_call_target="tpu_custom_call" | custom-call | flops 6039797760 | bytes 15728640 | tf_op jit(solution)/shard_map/grad_parts/pallas_call | solution.py:71
  20.2 1.4 collective-permute-start.1
  21.7 20.5 %stat_parts.1 = (f32[512,1024]{1,0:T(8,128)}, f32[512,1024]{1,0:T(8,128)}) custom-call(s32[1]{0:T(128)} %bitcast.core_ref, f32[3072,1024]{1,0:T(8,128)} %a_ref.3), custom_call_target="tpu_custom_call" | custom-call | flops 12884901888 | bytes 12582912 | tf_op jit(solution)/shard_map/stat_parts/pallas_call | solution.py:118
  42.4 26.2 %all_to_all.15 = f32[64,24,128]{2,1,0:T(8,128)S(1)} all-to-all(f32[64,24,128]{2,1,0:T(8,128)S(1)} %add.22), channel_id=1, replica_groups=mesh['x'=4,'zl'=2,'co'=2,'y'=4,'zh'=2] {'x','zl','y','zh'}, dimensions={0} | all-to-all | bytes 1572864 | tf_op jit(solution)/shard_map/all_to_all | solution.py:190
  68.8 2.5 %collective-permute-done.2 = f32[1,1,1,1,1,16,128]{6,5,4,3,2,1,0:T(8,128)S(1)} collective-permute-done((f32[1,1,1,1,1,16,128]{6,5,4,3,2,1,0:T(8,128)S(1)}, f32[1,1,1,1,1,16,128]{6,5,4,3,2,1,0:T(8,128)S(1)}, u32[]{:S(2)}, u32[]{:S(2)}) %collective-permute-start.2) | collective-permute-done | bytes 8224 | tf_op jit(solution)/shard_map/ppermute | solution.py:172
  72.0 3.1 %collective-permute-done.3 = f32[1,2,1,1,1,16,128]{6,5,4,3,2,1,0:T(8,128)S(1)} collective-permute-done((f32[1,2,1,1,1,16,128]{6,5,4,3,2,1,0:T(8,128)S(1)}, f32[1,2,1,1,1,16,128]{6,5,4,3,2,1,0:T(8,128)S(1)}, u32[]{:S(2)}, u32[]{:S(2)}) %collective-permute-start.3) | collective-permute-done | bytes 16416 | tf_op jit(solution)/shard_map/ppermute | solution.py:172
  75.1 0.7 collective-permute-start.4
  75.7 3.3 %add_bitcast_fusion = f32[64,8,1024]{2,1,0:T(8,128)} fusion(f32[512,1024]{1,0:T(8,128)S(1)} %copy-done, f32[512,1024]{1,0:T(8,128)} %collective-permute-done), kind=kLoop, calls=%fused_computation | loop fusion | flops 524288 | bytes 6291456 | tf_op jit(solution)/shard_map/reshape | solution.py:194
  79.0 5.0 %all-to-all-start = ((f32[64,8,1024]{2,1,0:T(8,128)}), f32[64,8,1024]{2,1,0:T(8,128)S(1)}, u32[]{:S(2)}, u32[]{:S(2)}) async-start(f32[64,8,1024]{2,1,0:T(8,128)} %add_bitcast_fusion), calls=%async_computation | async-start | bytes 4194304 | tf_op jit(solution)/shard_map/all_to_all | solution.py:194
  84.1 2.3 %collective-permute-start.5 = (f32[1,2,1,2,2,16,128]{6,5,4,3,2,1,0:T(8,128)S(1)}, f32[1,2,1,2,2,16,128]{6,5,4,3,2,1,0:T(8,128)S(1)}, u32[]{:S(2)}, u32[]{:S(2)}) collective-permute-start(f32[1,2,1,2,2,16,128]{6,5,4,3,2,1,0:T(8,128)S(1)} %pad_maximum_fusion.4), channel_id=1, source_target_pairs={{0,6},{1,7},{2,4},{3,5},{4,2},{5,3},{6,0},{7,1},{8,14},{9,15},{10,... | collective-permute-start | bytes 196616 | tf_op jit(solution)/shard_map/ppermute | solution.py:172
  86.4 9.6 %collective-permute-done.5 = f32[1,2,1,2,2,16,128]{6,5,4,3,2,1,0:T(8,128)S(1)} collective-permute-done((f32[1,2,1,2,2,16,128]{6,5,4,3,2,1,0:T(8,128)S(1)}, f32[1,2,1,2,2,16,128]{6,5,4,3,2,1,0:T(8,128)S(1)}, u32[]{:S(2)}, u32[]{:S(2)}) %collective-permute-start.5) | collective-permute-done | bytes 65568 | tf_op jit(solution)/shard_map/ppermute | solution.py:172
  96.0 7.3 %collective-permute-start.6 = (f32[1,2,1,4,2,16,128]{6,5,4,3,2,1,0:T(8,128)S(1)}, f32[1,2,1,4,2,16,128]{6,5,4,3,2,1,0:T(8,128)S(1)}, u32[]{:S(2)}, u32[]{:S(2)}) collective-permute-start(f32[1,2,1,4,2,16,128]{6,5,4,3,2,1,0:T(8,128)S(1)} %pad_maximum_fusion.3), channel_id=1, source_target_pairs={{0,32},{1,33},{2,34},{3,35},{4,36},{5,37},{6,38},{7,39},{8,40},{9,... | collective-permute-start | bytes 393224 | tf_op jit(solution)/shard_map/ppermute | solution.py:172
  103.3 6.9 %collective-permute-done.6 = f32[1,2,1,4,2,16,128]{6,5,4,3,2,1,0:T(8,128)S(1)} collective-permute-done((f32[1,2,1,4,2,16,128]{6,5,4,3,2,1,0:T(8,128)S(1)}, f32[1,2,1,4,2,16,128]{6,5,4,3,2,1,0:T(8,128)S(1)}, u32[]{:S(2)}, u32[]{:S(2)}) %collective-permute-start.6) | collective-permute-done | bytes 131104 | tf_op jit(solution)/shard_map/ppermute | solution.py:172
  110.3 6.3 %collective-permute-start.7 = (f32[2,2,1,4,2,16,128]{6,5,4,3,2,1,0:T(8,128)S(1)}, f32[2,2,1,4,2,16,128]{6,5,4,3,2,1,0:T(8,128)S(1)}, u32[]{:S(2)}, u32[]{:S(2)}) collective-permute-start(f32[2,2,1,4,2,16,128]{6,5,4,3,2,1,0:T(8,128)S(1)} %pad_maximum_fusion.2), channel_id=1, source_target_pairs={{0,96},{1,97},{2,98},{3,99},{4,100},{5,101},{6,102},{7,103},{8,104... | collective-permute-start | bytes 786440 | tf_op jit(solution)/shard_map/ppermute | solution.py:172
  116.6 4.7 %collective-permute-done.7 = f32[2,2,1,4,2,16,128]{6,5,4,3,2,1,0:T(8,128)S(1)} collective-permute-done((f32[2,2,1,4,2,16,128]{6,5,4,3,2,1,0:T(8,128)S(1)}, f32[2,2,1,4,2,16,128]{6,5,4,3,2,1,0:T(8,128)S(1)}, u32[]{:S(2)}, u32[]{:S(2)}) %collective-permute-start.7) | collective-permute-done | bytes 262176 | tf_op jit(solution)/shard_map/ppermute | solution.py:172
  121.3 0.9 pad_maximum_fusion.1
  122.1 2.6 %collective-permute-start.8 = (f32[4,2,1,4,2,16,128]{6,5,4,3,2,1,0:T(8,128)}, f32[4,2,1,4,2,16,128]{6,5,4,3,2,1,0:T(8,128)S(1)}, u32[]{:S(2)}, u32[]{:S(2)}) collective-permute-start(f32[4,2,1,4,2,16,128]{6,5,4,3,2,1,0:T(8,128)} %pad_maximum_fusion.1), channel_id=1, source_target_pairs={{0,8},{1,9},{2,10},{3,11},{4,12},{5,13},{6,14},{7,15},{8,0},{9,1},... | collective-permute-start | bytes 1572872 | tf_op jit(solution)/shard_map/ppermute | solution.py:172
  124.8 1.7 %slice.23 = f32[16,16,256]{2,1,0:T(8,128)} slice(f32[16,64,256]{2,1,0:T(8,128)} %bitcast.24), slice={[0:16], [0:16], [0:256]} | slice | bytes 524288 | tf_op jit(solution)/shard_map/slice | solution.py:186
  126.6 0.7 broadcast_in_dim.2
  127.3 5.4 %all-to-all-start.2 = ((f32[8,8,1152]{2,1,0:T(8,128)}), f32[8,8,1152]{2,1,0:T(8,128)S(1)}, u32[]{:S(2)}, u32[]{:S(2)}) async-start(f32[8,8,1152]{2,1,0:T(8,128)} %broadcast_in_dim.2), calls=%async_computation.2 | async-start | bytes 589824 | tf_op jit(solution)/shard_map/all_to_all | solution.py:208
  132.9 1.1 pad_maximum_fusion
  134.1 3.0 %final.1 = f32[64,256]{1,0:T(8,128)} custom-call(f32[64,1024]{1,0:T(8,128)} %inv_a_ref.1, f32[128,16,128]{2,1,0:T(8,128)} %bitcast.21, f32[256,256]{1,0:T(8,128)} %bitcast.22), custom_call_target="tpu_custom_call" | custom-call | tf_op jit(solution)/shard_map/final/pallas_call | solution.py:142
  137.1 4.3 %all-to-all-done.2 = f32[8,8,1152]{2,1,0:T(8,128)S(1)} async-done(((f32[8,8,1152]{2,1,0:T(8,128)}), f32[8,8,1152]{2,1,0:T(8,128)S(1)}, u32[]{:S(2)}, u32[]{:S(2)}) %all-to-all-start.2) | async-done | bytes 294944 | tf_op jit(solution)/shard_map/all_to_all | solution.py:208
  142.0 0.7 fusion.1
  (45 shorter events, 2.1 us)
Async XLA Ops:
  7.2 117.6 %all-gather.3.cloned.1.call-start = ((), (), s32[]{:S(2)}) async-start(), calls=%async_computation.3 | async-start | bytes 1114112 | tf_op jit(solution)/shard_map/all_gather | solution.py:186
  20.2 22.1 %copy-start.1 = (f32[64,24,128]{2,1,0:T(8,128)S(1)}, f32[64,24,128]{2,1,0:T(8,128)}, u32[]{:S(2)}) copy-start(f32[64,24,128]{2,1,0:T(8,128)} %get-tuple-element.9) | copy-start | bytes 2359300
  20.2 22.0 %collective-permute-start.1 = (f32[64,24,128]{2,1,0:T(8,128)}, f32[64,24,128]{2,1,0:T(8,128)S(1)}, u32[]{:S(2)}, u32[]{:S(2)}) collective-permute-start(f32[64,24,128]{2,1,0:T(8,128)} %get-tuple-element.10), channel_id=1, source_target_pairs={{0,8},{1,9},{2,10},{3,11},{4,12},{5,13},{6,14},{7,15},{8,0},{9,1},... | collective-permute-start | bytes 2359304 | tf_op jit(solution)/shard_map/ppermute | solution.py:172
  42.2 33.5 %collective-permute-start = (f32[512,1024]{1,0:T(8,128)}, f32[512,1024]{1,0:T(8,128)}, u32[]{:S(2)}, u32[]{:S(2)}) collective-permute-start(f32[512,1024]{1,0:T(8,128)} %get-tuple-element.8), channel_id=1, source_target_pairs={{0,8},{1,9},{2,10},{3,11},{4,12},{5,13},{6,14},{7,15},{8,0},{9,1},... | collective-permute-start | bytes 6291464 | tf_op jit(solution)/shard_map/ppermute | solution.py:172
  42.3 29.0 %copy-start.4 = (f32[16,256]{1,0:T(8,128)S(1)}, f32[16,256]{1,0:T(8,128)}, u32[]{:S(2)}) copy-start(f32[16,256]{1,0:T(8,128)} %param.11) | copy-start | bytes 49156
  42.3 33.5 %copy-start = (f32[512,1024]{1,0:T(8,128)S(1)}, f32[512,1024]{1,0:T(8,128)}, u32[]{:S(2)}) copy-start(f32[512,1024]{1,0:T(8,128)} %get-tuple-element.7) | copy-start | bytes 6291460
  68.6 56.1 %copy-start.3 = (f32[24,128]{1,0:T(8,128)}, f32[24,128]{1,0:T(8,128)S(1)}, u32[]{:S(2)}) copy-start(f32[24,128]{1,0:T(8,128)S(1)} %reduce_sum.19) | copy-start | bytes 36868
  68.7 2.6 %collective-permute-start.2 = (f32[1,1,1,1,1,16,128]{6,5,4,3,2,1,0:T(8,128)S(1)}, f32[1,1,1,1,1,16,128]{6,5,4,3,2,1,0:T(8,128)S(1)}, u32[]{:S(2)}, u32[]{:S(2)}) collective-permute-start(f32[1,1,1,1,1,16,128]{6,5,4,3,2,1,0:T(8,128)S(1)} %slice_bitcast_fusion), channel_id=1, source_target_pairs={{0,16},{1,17},{2,18},{3,19},{4,20},{5,21},{6,22},{7,23},{8,24},{9,... | collective-permute-start | bytes 24584 | tf_op jit(solution)/shard_map/ppermute | solution.py:172
  71.3 3.8 %collective-permute-start.3 = (f32[1,2,1,1,1,16,128]{6,5,4,3,2,1,0:T(8,128)S(1)}, f32[1,2,1,1,1,16,128]{6,5,4,3,2,1,0:T(8,128)S(1)}, u32[]{:S(2)}, u32[]{:S(2)}) collective-permute-start(f32[1,2,1,1,1,16,128]{6,5,4,3,2,1,0:T(8,128)S(1)} %pad_maximum_fusion.7), channel_id=1, source_target_pairs={{0,17},{1,16},{2,19},{3,18},{4,21},{5,20},{6,23},{7,22},{8,25},{9,... | collective-permute-start | bytes 49160 | tf_op jit(solution)/shard_map/ppermute | solution.py:172
  75.1 9.0 %collective-permute-start.4 = (f32[1,2,1,1,2,16,128]{6,5,4,3,2,1,0:T(8,128)S(1)}, f32[1,2,1,1,2,16,128]{6,5,4,3,2,1,0:T(8,128)S(1)}, u32[]{:S(2)}, u32[]{:S(2)}) collective-permute-start(f32[1,2,1,1,2,16,128]{6,5,4,3,2,1,0:T(8,128)S(1)} %pad_maximum_fusion.6), channel_id=1, source_target_pairs={{0,2},{1,3},{2,0},{3,1},{4,6},{5,7},{6,4},{7,5},{8,10},{9,11},{10,... | collective-permute-start | bytes 98312 | tf_op jit(solution)/shard_map/ppermute | solution.py:172
  79.0 47.4 %all-to-all-start = ((f32[64,8,1024]{2,1,0:T(8,128)}), f32[64,8,1024]{2,1,0:T(8,128)S(1)}, u32[]{:S(2)}, u32[]{:S(2)}) async-start(f32[64,8,1024]{2,1,0:T(8,128)} %add_bitcast_fusion), calls=%async_computation | async-start | bytes 4194304 | tf_op jit(solution)/shard_map/all_to_all | solution.py:194
  84.1 11.9 %collective-permute-start.5 = (f32[1,2,1,2,2,16,128]{6,5,4,3,2,1,0:T(8,128)S(1)}, f32[1,2,1,2,2,16,128]{6,5,4,3,2,1,0:T(8,128)S(1)}, u32[]{:S(2)}, u32[]{:S(2)}) collective-permute-start(f32[1,2,1,2,2,16,128]{6,5,4,3,2,1,0:T(8,128)S(1)} %pad_maximum_fusion.4), channel_id=1, source_target_pairs={{0,6},{1,7},{2,4},{3,5},{4,2},{5,3},{6,0},{7,1},{8,14},{9,15},{10,... | collective-permute-start | bytes 196616 | tf_op jit(solution)/shard_map/ppermute | solution.py:172
  96.0 14.2 %collective-permute-start.6 = (f32[1,2,1,4,2,16,128]{6,5,4,3,2,1,0:T(8,128)S(1)}, f32[1,2,1,4,2,16,128]{6,5,4,3,2,1,0:T(8,128)S(1)}, u32[]{:S(2)}, u32[]{:S(2)}) collective-permute-start(f32[1,2,1,4,2,16,128]{6,5,4,3,2,1,0:T(8,128)S(1)} %pad_maximum_fusion.3), channel_id=1, source_target_pairs={{0,32},{1,33},{2,34},{3,35},{4,36},{5,37},{6,38},{7,39},{8,40},{9,... | collective-permute-start | bytes 393224 | tf_op jit(solution)/shard_map/ppermute | solution.py:172
  110.3 11.0 %collective-permute-start.7 = (f32[2,2,1,4,2,16,128]{6,5,4,3,2,1,0:T(8,128)S(1)}, f32[2,2,1,4,2,16,128]{6,5,4,3,2,1,0:T(8,128)S(1)}, u32[]{:S(2)}, u32[]{:S(2)}) collective-permute-start(f32[2,2,1,4,2,16,128]{6,5,4,3,2,1,0:T(8,128)S(1)} %pad_maximum_fusion.2), channel_id=1, source_target_pairs={{0,96},{1,97},{2,98},{3,99},{4,100},{5,101},{6,102},{7,103},{8,104... | collective-permute-start | bytes 786440 | tf_op jit(solution)/shard_map/ppermute | solution.py:172
  122.1 10.6 %collective-permute-start.8 = (f32[4,2,1,4,2,16,128]{6,5,4,3,2,1,0:T(8,128)}, f32[4,2,1,4,2,16,128]{6,5,4,3,2,1,0:T(8,128)S(1)}, u32[]{:S(2)}, u32[]{:S(2)}) collective-permute-start(f32[4,2,1,4,2,16,128]{6,5,4,3,2,1,0:T(8,128)} %pad_maximum_fusion.1), channel_id=1, source_target_pairs={{0,8},{1,9},{2,10},{3,11},{4,12},{5,13},{6,14},{7,15},{8,0},{9,1},... | collective-permute-start | bytes 1572872 | tf_op jit(solution)/shard_map/ppermute | solution.py:172
  124.8 1.8 %slice-start = ((f32[24,128]{1,0:T(8,128)}), f32[8,128]{1,0:T(8,128)S(1)}, s32[]{:S(2)}) async-start(f32[24,128]{1,0:T(8,128)} %copy-done.3), calls=%async_computation.4 | async-start | bytes 8192 | tf_op jit(solution)/shard_map/slice | solution.py:206
  127.3 14.0 %all-to-all-start.2 = ((f32[8,8,1152]{2,1,0:T(8,128)}), f32[8,8,1152]{2,1,0:T(8,128)S(1)}, u32[]{:S(2)}, u32[]{:S(2)}) async-start(f32[8,8,1152]{2,1,0:T(8,128)} %broadcast_in_dim.2), calls=%async_computation.2 | async-start | bytes 589824 | tf_op jit(solution)/shard_map/all_to_all | solution.py:208
  132.9 8.5 %copy-start.5 = (f32[16,256]{1,0:T(8,128)S(1)}, f32[16,256]{1,0:T(8,128)}, u32[]{:S(2)}) copy-start(f32[16,256]{1,0:T(8,128)} %param.9) | copy-start | bytes 49156
  132.9 9.1 %copy-start.2 = (f32[64,1024]{1,0:T(8,128)S(1)}, f32[64,1024]{1,0:T(8,128)}, u32[]{:S(2)}) copy-start(f32[64,1024]{1,0:T(8,128)} %param.8) | copy-start | bytes 786436
Sparse Core Ops, SparseCore 0:
  72.1 48.0 all-gather.2

commit v2 on v1

--- a/solution.py
+++ b/solution.py
@@ -13,7 +13,8 @@
 SUB = ("x", "zl", "co", "y", "zh")
 SIZES = (4, 2, 2, 4, 2)
 CHIPS = ("x", "zl", "y", "zh")
-VMEM = 58 * 2**20
+CHUNKS = 6
+DEPTH = 2
 
 
 def split(block):
@@ -29,103 +30,120 @@
     return gram(lh, rh) + gram(lh, rl) + gram(ll, rh)
 
 
-def grad_kernel(core_ref, a_ref, g_ref, mine_ref, other_ref, grad, small):
-    step = pl.program_id(0)
-    gh, gl = split(g_ref[...])
-    ah, al = split(a_ref[...])
-
-    @pl.when(step == 0)
-    def _():
-        grad[...] = jnp.zeros_like(grad)
-        small[...] = jnp.zeros_like(small)
-
-    for j in range(0, grad.shape[0], 256):
-        c = slice(j, j + 256)
-        grad[c, :] += gram3(ah[:, c], al[:, c], gh, gl)
-    small[...] += gram3(gh, gl, gh, gl)
-
-    @pl.when(step == pl.num_programs(0) - 1)
-    def _():
-        core = core_ref[0]
-        for which, out in ((core, mine_ref), (1 - core, other_ref)):
-            for q in range(8):
-                owner = 2 * q + which
-                rows = pl.ds(pl.multiple_of(owner * 64, 64), 64)
-                for half in range(2):
-                    cols = slice(half * 128, half * 128 + 128)
-                    tile = slice(half * 8, half * 8 + 8)
-                    out[q * 8 : q * 8 + 8, tile, :] = grad[rows, cols].reshape(8, 8, 128)
-                for y in range(4):
-                    srows = pl.ds(pl.multiple_of(owner * 16 + 8 * (y // 2), 8), 8)
-                    part = small[srows, 128 * (y % 2) : 128 * (y % 2) + 128]
-                    out[q * 8 + 2 * y, 16:24, :] = part
-                    out[q * 8 + 2 * y + 1, 16:24, :] = part
+def grad_kernel(core_ref, a_hbm, g_hbm, mine_ref, other_ref, abuf, gbuf, grad, small, sems):
+    rows, cin = abuf.shape
+    tile = rows // CHUNKS
+    copies = []
+    for k in range(CHUNKS):
+        r = slice(k * tile, k * tile + tile)
+        copies.append(
+            (
+                pltpu.make_async_copy(g_hbm.at[r], gbuf.at[r], sems.at[2 * k]),
+                pltpu.make_async_copy(a_hbm.at[r], abuf.at[r], sems.at[2 * k + 1]),
+            )
+        )
+    for k in range(DEPTH):
+        for copy in copies[k]:
+            copy.start()
+    for k in range(CHUNKS):
+        r = slice(k * tile, k * tile + tile)
+        for copy in copies[k]:
+            copy.wait()
+        if k + DEPTH < CHUNKS:
+            for copy in copies[k + DEPTH]:
+                copy.start()
+        gh, gl = split(gbuf[r, :])
+        ah, al = split(abuf[r, :])
+        for j in range(0, cin, 256):
+            c = slice(j, j + 256)
+            part = gram3(ah[:, c], al[:, c], gh, gl)
+            grad[c, :] = part if k == 0 else grad[c, :] + part
+        part = gram3(gh, gl, gh, gl)
+        small[...] = part if k == 0 else small[...] + part
+
+    core = core_ref[0]
+    for which, out in ((core, mine_ref), (1 - core, other_ref)):
+        for q in range(8):
+            owner = 2 * q + which
+            own = pl.ds(pl.multiple_of(owner * 64, 64), 64)
+            for half in range(2):
+                cols = slice(half * 128, half * 128 + 128)
+                place = slice(half * 8, half * 8 + 8)
+                out[q * 8 : q * 8 + 8, place, :] = grad[own, cols].reshape(8, 8, 128)
+            for y in range(4):
+                srows = pl.ds(pl.multiple_of(owner * 16 + 8 * (y // 2), 8), 8)
+                part = small[srows, 128 * (y % 2) : 128 * (y % 2) + 128]
+                out[q * 8 + 2 * y, 16:24, :] = part
+                out[q * 8 + 2 * y + 1, 16:24, :] = part
 
 
 def grad_parts(core, activations, out_grads):
     rows, cin = activations.shape
     cout = out_grads.shape[1]
-    tile = 512
     shape = jax.ShapeDtypeStruct((64, 24, 128), F32)
-    spec = pl.BlockSpec((64, 24, 128), lambda k: (0, 0, 0))
+    hbm = pl.BlockSpec(memory_space=pltpu.HBM)
+    vmem = pl.BlockSpec(memory_space=pltpu.VMEM)
     return pl.pallas_call(
         grad_kernel,
-        grid=(rows // tile,),
-        in_specs=[
-            pl.BlockSpec(memory_space=pltpu.SMEM),
-            pl.BlockSpec((tile, cin), lambda k: (k, 0)),
-            pl.BlockSpec((tile, cout), lambda k: (k, 0)),
+        in_specs=[pl.BlockSpec(memory_space=pltpu.SMEM), hbm, hbm],
+        out_specs=[vmem] * 2,
+        out_shape=[shape, shape],
+        scratch_shapes=[
+            pltpu.VMEM((rows, cin), F32),
+            pltpu.VMEM((rows, cout), F32),
+            pltpu.VMEM((cin, cout), F32),
+            pltpu.VMEM((cout, cout), F32),
+            pltpu.SemaphoreType.DMA((2 * CHUNKS,)),
         ],
-        out_specs=[spec, spec],
-        out_shape=[shape, shape],
-        scratch_shapes=[pltpu.VMEM((cin, cout), F32), pltpu.VMEM((cout, cout), F32)],
-        compiler_params=pltpu.CompilerParams(vmem_limit_bytes=VMEM),
+        compiler_params=pltpu.CompilerParams(vmem_limit_bytes=56 * 2**20),
         cost_estimate=pl.CostEstimate(flops=6 * rows * (cin + cout) * cout, bytes_accessed=4 * rows * (cin + cout), transcendentals=0),
         name="grad_parts",
     )(core, activations, out_grads)
 
 
-def stat_kernel(core_ref, a_ref, mine_ref, other_ref, acc):
-    step = pl.program_id(0)
+def stat_kernel(core_ref, a_hbm, mine_ref, other_ref, buf, ah, al, acc, sems):
     cin = acc.shape[0]
-    ah, al = split(a_ref[...])
-
-    @pl.when(step == 0)
-    def _():
-        acc[...] = jnp.zeros_like(acc)
-
-    for i in range(0, cin, 256):
-        ci, cj = slice(i, i + 256), slice(i, cin)
-        acc[ci, cj] += gram3(ah[:, ci], al[:, ci], ah[:, cj], al[:, cj])
-
-    @pl.when(step == pl.num_programs(0) - 1)
-    def _():
-        for i in range(0, cin, 256):
-            for j in range(i + 256, cin, 256):
-                acc[j : j + 256, i : i + 256] = acc[i : i + 256, j : j + 256].T
-        core = core_ref[0]
-        for which, out in ((core, mine_ref), (1 - core, other_ref)):
-            for q in range(8):
-                rows = pl.ds(pl.multiple_of((2 * q + which) * 64, 64), 64)
-                out[q * 64 : q * 64 + 64, :] = acc[rows, :]
+    count = cin // 256
+    copies = [
+        pltpu.make_async_copy(a_hbm.at[:, j * 256 : j * 256 + 256], buf.at[j], sems.at[j]) for j in range(count)
+    ]
+    for copy in copies[:DEPTH]:
+        copy.start()
+    for j in range(count):
+        copies[j].wait()
+        if j + DEPTH < count:
+            copies[j + DEPTH].start()
+        cj = slice(j * 256, j * 256 + 256)
+        ah[:, cj], al[:, cj] = split(buf[j])
+        for i in range(j + 1):
+            ci = slice(i * 256, i * 256 + 256)
+            acc[ci, cj] = gram3(ah[:, ci], al[:, ci], ah[:, cj], al[:, cj])
+            if i < j:
+                acc[cj, ci] = acc[ci, cj].T
+    core = core_ref[0]
+    for which, out in ((core, mine_ref), (1 - core, other_ref)):
+        for q in range(8):
+            own = pl.ds(pl.multiple_of((2 * q + which) * 64, 64), 64)
+            out[q * 64 : q * 64 + 64, :] = acc[own, :]
 
 
 def stat_parts(core, activations):
     rows, cin = activations.shape
-    tile = 512
     shape = jax.ShapeDtypeStruct((cin // 2, cin), F32)
-    spec = pl.BlockSpec((cin // 2, cin), lambda k: (0, 0))
+    vmem = pl.BlockSpec(memory_space=pltpu.VMEM)
     return pl.pallas_call(
         stat_kernel,
-        grid=(rows // tile,),
-        in_specs=[
-            pl.BlockSpec(memory_space=pltpu.SMEM),
-            pl.BlockSpec((tile, cin), lambda k: (k, 0)),
+        in_specs=[pl.BlockSpec(memory_space=pltpu.SMEM), pl.BlockSpec(memory_space=pltpu.HBM)],
+        out_specs=[vmem, vmem],
+        out_shape=[shape, shape],
+        scratch_shapes=[
+            pltpu.VMEM((cin // 256, rows, 256), F32),
+            pltpu.VMEM((rows, cin), BF16),
+            pltpu.VMEM((rows, cin), BF16),
+            pltpu.VMEM((cin, cin), F32),
+            pltpu.SemaphoreType.DMA((cin // 256,)),
         ],
-        out_specs=[spec, spec],
-        out_shape=[shape, shape],
-        scratch_shapes=[pltpu.VMEM((cin, cin), F32)],
-        compiler_params=pltpu.CompilerParams(vmem_limit_bytes=VMEM),
+        compiler_params=pltpu.CompilerParams(vmem_limit_bytes=52 * 2**20),
         cost_estimate=pl.CostEstimate(flops=4 * rows * cin * cin, bytes_accessed=4 * rows * cin, transcendentals=0),
         name="stat_parts",
     )(core, activations)
@@ -142,7 +160,7 @@
     return pl.pallas_call(
         final_kernel,
         out_shape=jax.ShapeDtypeStruct((inverse_a.shape[0], 256), F32),
-        compiler_params=pltpu.CompilerParams(vmem_limit_bytes=VMEM),
+        compiler_params=pltpu.CompilerParams(vmem_limit_bytes=16 * 2**20),
         name="final",
     )(inverse_a, grad, inverse_g)
 
@@ -187,8 +205,10 @@
 
     g_mine, g_other = grad_parts(core, activations, out_grads)
     g_sum = g_mine + move(g_other, CORE)
+    g_sum, core = lax.optimization_barrier((g_sum, core))
     g_all = lax.all_to_all(g_sum, CHIPS, 0, 0, tiled=True)
     s_mine, s_other = stat_parts(core, activations)
+    g_all, s_mine, s_other = lax.optimization_barrier((g_all, s_mine, s_other))
     s_sum = s_mine + move(s_other, CORE)
     g_own = jnp.sum(g_all, axis=0)
     s_all = lax.all_to_all(s_sum.reshape(64, 8, 1024), CHIPS, 0, 0, tiled=True)

time: 150 us -> 142 us (0.947)
  blocking collectives: 26.2 us -> 0 us
  starting transfers between devices: 31.2 us -> 53.4 us
  Pallas kernels: 36.6 us -> 33.2 us
    all_to_all x1 -> x0, blocking collectives: 26.2 us -> none  [local(): g_all = lax.all_to_all(g_sum, CHIPS, 0, 0, tiled=True)]
    all_to_all x0 -> x1, starting transfers between devices: none -> 11.2 us  [local(): g_all = lax.all_to_all(g_sum, CHIPS, 0, 0, tiled=True)]
    ppermute x9, starting transfers between devices: 20.7 us -> 27.6 us  [move(): return lax.ppermute(array, SUB, table)]
    all_to_all x1, starting transfers between devices: 5.02 us -> 9.4 us  [local(): s_all = lax.all_to_all(s_sum.reshape(64, 8, 1024), CHIPS, 0, 0, tiled=True)]
    ppermute x9, waiting for transfers between devices: 26.8 us -> 23.8 us  [move(): return lax.ppermute(array, SUB, table)]
    pallas_call x2, Pallas kernels: 33.6 us -> 31.5 us  [the longest x1 19.7 us: stat_parts(): pl.pallas_call(stat_kernel, in_specs=[pl.BlockSpec(memory_space=pltpu.SME...]
    add x1, other arithmetic: 0.08 us -> 2.1 us  [local(): g_sum = g_mine + move(g_other, CORE)]
    all_to_all x1, waiting for transfers between devices: 4.27 us -> 5.95 us  [local(): rows = lax.all_to_all(spread, ('y', 'zh'), 0, 0, tiled=True)]
  transfers between devices with their start and end apart: 12 -> 13, of which waited for: 6 -> 7; matrix products, arithmetic and copies ran while one was open for 6% -> 5% of each run, Pallas kernels for 16% -> 15%
where the time goes in v2:
time: 142 us
  starting transfers between devices  53.4 us (38%)
  Pallas kernels  33.2 us (23%)
  waiting for transfers between devices  29.8 us (21%)
  between operations  14.2 us (10%)
  other arithmetic  8.2 us (6%)
  local copies, waits for them, and re-layouts  3.09 us (2%)
    ppermute x9, starting transfers between devices, move(): return lax.ppermute(array, SUB, table)  27.6 us
    ppermute x9, waiting for transfers between devices, move(): return lax.ppermute(array, SUB, table)  23.8 us
    pallas_call x1, Pallas kernels, stat_parts(): pl.pallas_call(stat_kernel, in_specs=[pl.BlockSpec(memory_space=pltpu.SME...  19.7 us
    pallas_call x1, Pallas kernels, grad_parts(): pl.pallas_call(grad_kernel, in_specs=[pl.BlockSpec(memory_space=pltpu.SME...  11.9 us
    all_to_all x1, starting transfers between devices, local(): g_all = lax.all_to_all(g_sum, CHIPS, 0, 0, tiled=True)  11.2 us
    all_to_all x1, starting transfers between devices, local(): s_all = lax.all_to_all(s_sum.reshape(64, 8, 1024), CHIPS, 0, 0, tiled=True)  9.4 us
    all_to_all x1, waiting for transfers between devices, local(): rows = lax.all_to_all(spread, ('y', 'zh'), 0, 0, tiled=True)  5.95 us
    all_to_all x1, starting transfers between devices, local(): rows = lax.all_to_all(spread, ('y', 'zh'), 0, 0, tiled=True)  4.91 us
  transfers between devices with their start and end apart: 13, of which 7 were waited for; matrix products, arithmetic and copies ran while one was open for 5% of the time, Pallas kernels for 15%

profile of v2, /device:TPU:1, one launch (start us, length us, event | category | flops | bytes accessed | tf_op | source)
XLA Modules:
  0.0 141.9 jit_solution(18058123880113647262)
XLA Ops:
  7.2 11.9 %grad_parts.1 = (f32[64,24,128]{2,1,0:T(8,128)}, f32[64,24,128]{2,1,0:T(8,128)}) custom-call(s32[1]{0:T(128)} %bitcast.core_ref, f32[3072,1024]{1,0:T(8,128)} %a_hbm.3, f32[3072,256]{1,0:T(8,128)} %g_hbm.1), custom_call_target="tpu_custom_call" | custom-call | flops 6039797760 | bytes 15728640 | tf_op jit(solution)/shard_map/grad_parts/pallas_call | solution.py:86
  19.1 1.5 %collective-permute-start = (f32[64,24,128]{2,1,0:T(8,128)}, f32[64,24,128]{2,1,0:T(8,128)S(1)}, u32[]{:S(2)}, u32[]{:S(2)}) collective-permute-start(f32[64,24,128]{2,1,0:T(8,128)} %get-tuple-element.13), channel_id=1, source_target_pairs={{0,8},{1,9},{2,10},{3,11},{4,12},{5,13},{6,14},{7,15},{8,0},{9,1},... | collective-permute-start | bytes 2359304 | tf_op jit(solution)/shard_map/ppermute | solution.py:190
  20.6 2.1 %collective-permute-done = f32[64,24,128]{2,1,0:T(8,128)S(1)} collective-permute-done((f32[64,24,128]{2,1,0:T(8,128)}, f32[64,24,128]{2,1,0:T(8,128)S(1)}, u32[]{:S(2)}, u32[]{:S(2)}) %collective-permute-start) | collective-permute-done | bytes 786464 | tf_op jit(solution)/shard_map/ppermute | solution.py:190
  22.7 2.1 %add.21 = f32[64,24,128]{2,1,0:T(8,128)} add(f32[64,24,128]{2,1,0:T(8,128)} %get-tuple-element.12, f32[64,24,128]{2,1,0:T(8,128)S(1)} %collective-permute-done) | non-fusion elementwise | flops 196608 | bytes 2359296 | tf_op jit(solution)/shard_map/add | solution.py:207
  24.8 11.2 %all-to-all-start = ((f32[64,24,128]{2,1,0:T(8,128)}), f32[64,24,128]{2,1,0:T(8,128)S(1)}, u32[]{:S(2)}, u32[]{:S(2)}) async-start(f32[64,24,128]{2,1,0:T(8,128)} %add.21), calls=%async_computation | async-start | bytes 1572864 | tf_op jit(solution)/shard_map/all_to_all | solution.py:209
  36.3 19.7 %stat_parts.1 = (f32[512,1024]{1,0:T(8,128)}, f32[512,1024]{1,0:T(8,128)}) custom-call(s32[1]{0:T(128)} %bitcast.core_ref, f32[3072,1024]{1,0:T(8,128)} %a_hbm.3), custom_call_target="tpu_custom_call" | custom-call | flops 12884901888 | bytes 12582912 | tf_op jit(solution)/shard_map/stat_parts/pallas_call | solution.py:134
  56.8 1.4 collective-permute-start.2
  58.1 1.2 collective-permute-done.2
  59.4 2.5 %collective-permute-start.3 = (f32[1,2,1,1,1,16,128]{6,5,4,3,2,1,0:T(8,128)S(1)}, f32[1,2,1,1,1,16,128]{6,5,4,3,2,1,0:T(8,128)S(1)}, u32[]{:S(2)}, u32[]{:S(2)}) collective-permute-start(f32[1,2,1,1,1,16,128]{6,5,4,3,2,1,0:T(8,128)S(1)} %pad_maximum_fusion.7), channel_id=1, source_target_pairs={{0,17},{1,16},{2,19},{3,18},{4,21},{5,20},{6,23},{7,22},{8,25},{9,... | collective-permute-start | bytes 49160 | tf_op jit(solution)/shard_map/ppermute | solution.py:190
  63.2 1.4 collective-permute-start.4
  64.5 3.3 %add_bitcast_fusion = f32[64,8,1024]{2,1,0:T(8,128)} fusion(f32[512,1024]{1,0:T(8,128)} %get-tuple-element.18, f32[512,1024]{1,0:T(8,128)S(1)} %collective-permute-done.1), kind=kLoop, calls=%fused_computation | loop fusion | flops 524288 | bytes 6291456 | tf_op jit(solution)/shard_map/reshape | solution.py:214
  67.8 9.4 %all-to-all-start.1 = ((f32[64,8,1024]{2,1,0:T(8,128)}), f32[64,8,1024]{2,1,0:T(8,128)S(1)}, u32[]{:S(2)}, u32[]{:S(2)}) async-start(f32[64,8,1024]{2,1,0:T(8,128)} %add_bitcast_fusion), calls=%async_computation.1 | async-start | bytes 4194304 | tf_op jit(solution)/shard_map/all_to_all | solution.py:214
  77.3 2.3 %collective-permute-start.5 = (f32[1,2,1,2,2,16,128]{6,5,4,3,2,1,0:T(8,128)S(1)}, f32[1,2,1,2,2,16,128]{6,5,4,3,2,1,0:T(8,128)S(1)}, u32[]{:S(2)}, u32[]{:S(2)}) collective-permute-start(f32[1,2,1,2,2,16,128]{6,5,4,3,2,1,0:T(8,128)S(1)} %pad_maximum_fusion.4), channel_id=1, source_target_pairs={{0,6},{1,7},{2,4},{3,5},{4,2},{5,3},{6,0},{7,1},{8,14},{9,15},{10,... | collective-permute-start | bytes 196616 | tf_op jit(solution)/shard_map/ppermute | solution.py:190
  79.6 10.7 %collective-permute-done.5 = f32[1,2,1,2,2,16,128]{6,5,4,3,2,1,0:T(8,128)S(1)} collective-permute-done((f32[1,2,1,2,2,16,128]{6,5,4,3,2,1,0:T(8,128)S(1)}, f32[1,2,1,2,2,16,128]{6,5,4,3,2,1,0:T(8,128)S(1)}, u32[]{:S(2)}, u32[]{:S(2)}) %collective-permute-start.5) | collective-permute-done | bytes 65568 | tf_op jit(solution)/shard_map/ppermute | solution.py:190
  90.3 10.0 %collective-permute-start.6 = (f32[1,2,1,4,2,16,128]{6,5,4,3,2,1,0:T(8,128)S(1)}, f32[1,2,1,4,2,16,128]{6,5,4,3,2,1,0:T(8,128)S(1)}, u32[]{:S(2)}, u32[]{:S(2)}) collective-permute-start(f32[1,2,1,4,2,16,128]{6,5,4,3,2,1,0:T(8,128)S(1)} %pad_maximum_fusion.3), channel_id=1, source_target_pairs={{0,32},{1,33},{2,34},{3,35},{4,36},{5,37},{6,38},{7,39},{8,40},{9,... | collective-permute-start | bytes 393224 | tf_op jit(solution)/shard_map/ppermute | solution.py:190
  100.3 4.5 %collective-permute-done.6 = f32[1,2,1,4,2,16,128]{6,5,4,3,2,1,0:T(8,128)S(1)} collective-permute-done((f32[1,2,1,4,2,16,128]{6,5,4,3,2,1,0:T(8,128)S(1)}, f32[1,2,1,4,2,16,128]{6,5,4,3,2,1,0:T(8,128)S(1)}, u32[]{:S(2)}, u32[]{:S(2)}) %collective-permute-start.6) | collective-permute-done | bytes 131104 | tf_op jit(solution)/shard_map/ppermute | solution.py:190
  104.8 5.3 %collective-permute-start.7 = (f32[2,2,1,4,2,16,128]{6,5,4,3,2,1,0:T(8,128)S(1)}, f32[2,2,1,4,2,16,128]{6,5,4,3,2,1,0:T(8,128)S(1)}, u32[]{:S(2)}, u32[]{:S(2)}) collective-permute-start(f32[2,2,1,4,2,16,128]{6,5,4,3,2,1,0:T(8,128)S(1)} %pad_maximum_fusion.2), channel_id=1, source_target_pairs={{0,96},{1,97},{2,98},{3,99},{4,100},{5,101},{6,102},{7,103},{8,104... | collective-permute-start | bytes 786440 | tf_op jit(solution)/shard_map/ppermute | solution.py:190
  110.1 4.7 %collective-permute-done.7 = f32[2,2,1,4,2,16,128]{6,5,4,3,2,1,0:T(8,128)S(1)} collective-permute-done((f32[2,2,1,4,2,16,128]{6,5,4,3,2,1,0:T(8,128)S(1)}, f32[2,2,1,4,2,16,128]{6,5,4,3,2,1,0:T(8,128)S(1)}, u32[]{:S(2)}, u32[]{:S(2)}) %collective-permute-start.7) | collective-permute-done | bytes 262176 | tf_op jit(solution)/shard_map/ppermute | solution.py:190
  114.8 0.9 pad_maximum_fusion.1
  115.7 2.6 %collective-permute-start.8 = (f32[4,2,1,4,2,16,128]{6,5,4,3,2,1,0:T(8,128)}, f32[4,2,1,4,2,16,128]{6,5,4,3,2,1,0:T(8,128)S(1)}, u32[]{:S(2)}, u32[]{:S(2)}) collective-permute-start(f32[4,2,1,4,2,16,128]{6,5,4,3,2,1,0:T(8,128)} %pad_maximum_fusion.1), channel_id=1, source_target_pairs={{0,8},{1,9},{2,10},{3,11},{4,12},{5,13},{6,14},{7,15},{8,0},{9,1},... | collective-permute-start | bytes 1572872 | tf_op jit(solution)/shard_map/ppermute | solution.py:190
  118.3 1.0 slice.23
  120.2 4.9 %all-to-all-start.2 = ((f32[8,8,1152]{2,1,0:T(8,128)}), f32[8,8,1152]{2,1,0:T(8,128)S(1)}, u32[]{:S(2)}, u32[]{:S(2)}) async-start(f32[8,8,1152]{2,1,0:T(8,128)} %broadcast_in_dim.2), calls=%async_computation.2 | async-start | bytes 589824 | tf_op jit(solution)/shard_map/all_to_all | solution.py:228
  126.1 1.7 %final.1 = f32[64,256]{1,0:T(8,128)} custom-call(f32[64,1024]{1,0:T(8,128)S(1)} %copy-done, f32[128,16,128]{2,1,0:T(8,128)S(1)} %bitcast.21, f32[256,256]{1,0:T(8,128)S(1)} %bitcast.22), custom_call_target="tpu_custom_call" | custom-call | tf_op jit(solution)/shard_map/final/pallas_call | solution.py:160
  127.8 5.9 %all-to-all-done.2 = f32[8,8,1152]{2,1,0:T(8,128)S(1)} async-done(((f32[8,8,1152]{2,1,0:T(8,128)}), f32[8,8,1152]{2,1,0:T(8,128)S(1)}, u32[]{:S(2)}, u32[]{:S(2)}) %all-to-all-start.2) | async-done | bytes 294944 | tf_op jit(solution)/shard_map/all_to_all | solution.py:228
  (44 shorter events, 5.7 us)
Async XLA Ops:
  19.1 3.6 %collective-permute-start = (f32[64,24,128]{2,1,0:T(8,128)}, f32[64,24,128]{2,1,0:T(8,128)S(1)}, u32[]{:S(2)}, u32[]{:S(2)}) collective-permute-start(f32[64,24,128]{2,1,0:T(8,128)} %get-tuple-element.13), channel_id=1, source_target_pairs={{0,8},{1,9},{2,10},{3,11},{4,12},{5,13},{6,14},{7,15},{8,0},{9,1},... | collective-permute-start | bytes 2359304 | tf_op jit(solution)/shard_map/ppermute | solution.py:190
  24.8 31.1 %all-to-all-start = ((f32[64,24,128]{2,1,0:T(8,128)}), f32[64,24,128]{2,1,0:T(8,128)S(1)}, u32[]{:S(2)}, u32[]{:S(2)}) async-start(f32[64,24,128]{2,1,0:T(8,128)} %add.21), calls=%async_computation | async-start | bytes 1572864 | tf_op jit(solution)/shard_map/all_to_all | solution.py:209
  36.0 25.8 %copy-start.3 = (f32[16,256]{1,0:T(8,128)S(1)}, f32[16,256]{1,0:T(8,128)}, u32[]{:S(2)}) copy-start(f32[16,256]{1,0:T(8,128)} %param.11) | copy-start | bytes 49156
  36.0 82.3 %all-gather.3.cloned.1.call-start = ((), (), s32[]{:S(2)}) async-start(), calls=%async_computation.3 | async-start | bytes 1114112 | tf_op jit(solution)/shard_map/all_gather | solution.py:204
  55.9 8.6 %collective-permute-start.1 = (f32[512,1024]{1,0:T(8,128)}, f32[512,1024]{1,0:T(8,128)S(1)}, u32[]{:S(2)}, u32[]{:S(2)}) collective-permute-start(f32[512,1024]{1,0:T(8,128)} %get-tuple-element.19), channel_id=1, source_target_pairs={{0,8},{1,9},{2,10},{3,11},{4,12},{5,13},{6,14},{7,15},{8,0},{9,1},... | collective-permute-start | bytes 6291464 | tf_op jit(solution)/shard_map/ppermute | solution.py:190
  56.7 61.5 %copy-start.2 = (f32[24,128]{1,0:T(8,128)}, f32[24,128]{1,0:T(8,128)S(1)}, u32[]{:S(2)}) copy-start(f32[24,128]{1,0:T(8,128)S(1)} %reduce_sum.19) | copy-start | bytes 36868
  56.8 2.6 %collective-permute-start.2 = (f32[1,1,1,1,1,16,128]{6,5,4,3,2,1,0:T(8,128)S(1)}, f32[1,1,1,1,1,16,128]{6,5,4,3,2,1,0:T(8,128)S(1)}, u32[]{:S(2)}, u32[]{:S(2)}) collective-permute-start(f32[1,1,1,1,1,16,128]{6,5,4,3,2,1,0:T(8,128)S(1)} %slice_bitcast_fusion), channel_id=1, source_target_pairs={{0,16},{1,17},{2,18},{3,19},{4,20},{5,21},{6,22},{7,23},{8,24},{9,... | collective-permute-start | bytes 24584 | tf_op jit(solution)/shard_map/ppermute | solution.py:190
  59.4 3.8 %collective-permute-start.3 = (f32[1,2,1,1,1,16,128]{6,5,4,3,2,1,0:T(8,128)S(1)}, f32[1,2,1,1,1,16,128]{6,5,4,3,2,1,0:T(8,128)S(1)}, u32[]{:S(2)}, u32[]{:S(2)}) collective-permute-start(f32[1,2,1,1,1,16,128]{6,5,4,3,2,1,0:T(8,128)S(1)} %pad_maximum_fusion.7), channel_id=1, source_target_pairs={{0,17},{1,16},{2,19},{3,18},{4,21},{5,20},{6,23},{7,22},{8,25},{9,... | collective-permute-start | bytes 49160 | tf_op jit(solution)/shard_map/ppermute | solution.py:190
  63.2 14.1 %collective-permute-start.4 = (f32[1,2,1,1,2,16,128]{6,5,4,3,2,1,0:T(8,128)S(1)}, f32[1,2,1,1,2,16,128]{6,5,4,3,2,1,0:T(8,128)S(1)}, u32[]{:S(2)}, u32[]{:S(2)}) collective-permute-start(f32[1,2,1,1,2,16,128]{6,5,4,3,2,1,0:T(8,128)S(1)} %pad_maximum_fusion.6), channel_id=1, source_target_pairs={{0,2},{1,3},{2,0},{3,1},{4,6},{5,7},{6,4},{7,5},{8,10},{9,11},{10,... | collective-permute-start | bytes 98312 | tf_op jit(solution)/shard_map/ppermute | solution.py:190
  67.8 51.5 %all-to-all-start.1 = ((f32[64,8,1024]{2,1,0:T(8,128)}), f32[64,8,1024]{2,1,0:T(8,128)S(1)}, u32[]{:S(2)}, u32[]{:S(2)}) async-start(f32[64,8,1024]{2,1,0:T(8,128)} %add_bitcast_fusion), calls=%async_computation.1 | async-start | bytes 4194304 | tf_op jit(solution)/shard_map/all_to_all | solution.py:214
  77.3 13.0 %collective-permute-start.5 = (f32[1,2,1,2,2,16,128]{6,5,4,3,2,1,0:T(8,128)S(1)}, f32[1,2,1,2,2,16,128]{6,5,4,3,2,1,0:T(8,128)S(1)}, u32[]{:S(2)}, u32[]{:S(2)}) collective-permute-start(f32[1,2,1,2,2,16,128]{6,5,4,3,2,1,0:T(8,128)S(1)} %pad_maximum_fusion.4), channel_id=1, source_target_pairs={{0,6},{1,7},{2,4},{3,5},{4,2},{5,3},{6,0},{7,1},{8,14},{9,15},{10,... | collective-permute-start | bytes 196616 | tf_op jit(solution)/shard_map/ppermute | solution.py:190
  90.3 14.4 %collective-permute-start.6 = (f32[1,2,1,4,2,16,128]{6,5,4,3,2,1,0:T(8,128)S(1)}, f32[1,2,1,4,2,16,128]{6,5,4,3,2,1,0:T(8,128)S(1)}, u32[]{:S(2)}, u32[]{:S(2)}) collective-permute-start(f32[1,2,1,4,2,16,128]{6,5,4,3,2,1,0:T(8,128)S(1)} %pad_maximum_fusion.3), channel_id=1, source_target_pairs={{0,32},{1,33},{2,34},{3,35},{4,36},{5,37},{6,38},{7,39},{8,40},{9,... | collective-permute-start | bytes 393224 | tf_op jit(solution)/shard_map/ppermute | solution.py:190
  104.8 9.9 %collective-permute-start.7 = (f32[2,2,1,4,2,16,128]{6,5,4,3,2,1,0:T(8,128)S(1)}, f32[2,2,1,4,2,16,128]{6,5,4,3,2,1,0:T(8,128)S(1)}, u32[]{:S(2)}, u32[]{:S(2)}) collective-permute-start(f32[2,2,1,4,2,16,128]{6,5,4,3,2,1,0:T(8,128)S(1)} %pad_maximum_fusion.2), channel_id=1, source_target_pairs={{0,96},{1,97},{2,98},{3,99},{4,100},{5,101},{6,102},{7,103},{8,104... | collective-permute-start | bytes 786440 | tf_op jit(solution)/shard_map/ppermute | solution.py:190
  115.7 9.4 %collective-permute-start.8 = (f32[4,2,1,4,2,16,128]{6,5,4,3,2,1,0:T(8,128)}, f32[4,2,1,4,2,16,128]{6,5,4,3,2,1,0:T(8,128)S(1)}, u32[]{:S(2)}, u32[]{:S(2)}) collective-permute-start(f32[4,2,1,4,2,16,128]{6,5,4,3,2,1,0:T(8,128)} %pad_maximum_fusion.1), channel_id=1, source_target_pairs={{0,8},{1,9},{2,10},{3,11},{4,12},{5,13},{6,14},{7,15},{8,0},{9,1},... | collective-permute-start | bytes 1572872 | tf_op jit(solution)/shard_map/ppermute | solution.py:190
  118.3 1.1 slice-start
  120.2 13.5 %all-to-all-start.2 = ((f32[8,8,1152]{2,1,0:T(8,128)}), f32[8,8,1152]{2,1,0:T(8,128)S(1)}, u32[]{:S(2)}, u32[]{:S(2)}) async-start(f32[8,8,1152]{2,1,0:T(8,128)} %broadcast_in_dim.2), calls=%async_computation.2 | async-start | bytes 589824 | tf_op jit(solution)/shard_map/all_to_all | solution.py:228
  125.1 0.9 copy-start
  125.2 8.5 %copy-start.4 = (f32[16,256]{1,0:T(8,128)S(1)}, f32[16,256]{1,0:T(8,128)}, u32[]{:S(2)}) copy-start(f32[16,256]{1,0:T(8,128)} %param.9) | copy-start | bytes 49156
  125.3 9.1 %copy-start.1 = (f32[64,1024]{1,0:T(8,128)S(1)}, f32[64,1024]{1,0:T(8,128)}, u32[]{:S(2)}) copy-start(f32[64,1024]{1,0:T(8,128)} %param.8) | copy-start | bytes 786436
Sparse Core Ops, SparseCore 0:
  62.6 48.4 all-gather.2

commit v3 on v2

v3 whole, which is shorter than its diff:
```python
import jax
import jax.numpy as jnp
from jax import lax
from jax.experimental import pallas as pl
from jax.experimental.pallas import tpu as pltpu
from jax.sharding import PartitionSpec as P

decay_rate = 0.6
F32 = jnp.float32
BF16 = jnp.bfloat16
SUB = ("x", "zl", "co", "y", "zh")
SIZES = (4, 2, 2, 4, 2)
CHIPS = ("x", "zl", "y", "zh")
CHUNKS = 6
DEPTH = 2


def split(block):
    high = block.astype(BF16)
    return high, (block - high.astype(F32)).astype(BF16)


def gram(left, right):
    return lax.dot_general(left, right, (((0,), (0,)), ((), ())), preferred_element_type=F32)


def gram3(lh, ll, rh, rl):
    return gram(lh, rh) + gram(lh, rl) + gram(ll, rh)


def in_hbm():
    return pl.BlockSpec(memory_space=pltpu.HBM)


def in_vmem():
    return pl.BlockSpec(memory_space=pltpu.VMEM)


def in_smem():
    return pl.BlockSpec(memory_space=pltpu.SMEM)


def grad_kernel(core_ref, a_hbm, g_hbm, mine_ref, other_ref, abuf, gbuf, ah, al, gh, gl, grad, small, sems):
    rows, cin = abuf.shape
    tile = rows // CHUNKS
    copies = []
    for k in range(CHUNKS):
        r = slice(k * tile, k * tile + tile)
        copies.append(
            (
                pltpu.make_async_copy(g_hbm.at[r], gbuf.at[r], sems.at[2 * k]),
                pltpu.make_async_copy(a_hbm.at[r], abuf.at[r], sems.at[2 * k + 1]),
            )
        )

    def fetch(k):
        if k < CHUNKS:
            for copy in copies[k]:
                copy.start()

    def prepare(k):
        if k < CHUNKS:
            for copy in copies[k]:
                copy.wait()
            fetch(k + DEPTH)
            r = slice(k * tile, k * tile + tile)
            gh[k % 2], gl[k % 2] = split(gbuf[r, :])
            ah[k % 2], al[k % 2] = split(abuf[r, :])

    for k in range(DEPTH):
        fetch(k)
    prepare(0)
    for k in range(CHUNKS):
        prepare(k + 1)
        now = k % 2
        for j in range(0, cin, 256):
            c = slice(j, j + 256)
            part = gram3(ah[now, :, c], al[now, :, c], gh[now], gl[now])
            grad[c, :] = part if k == 0 else grad[c, :] + part
        part = gram3(gh[now], gl[now], gh[now], gl[now])
        small[...] = part if k == 0 else small[...] + part

    core = core_ref[0]
    for which, out in ((core, mine_ref), (1 - core, other_ref)):
        for q in range(8):
            owner = 2 * q + which
            own = pl.ds(pl.multiple_of(owner * 64, 64), 64)
            for half in range(2):
                cols = slice(half * 128, half * 128 + 128)
                place = slice(half * 8, half * 8 + 8)
                out[q * 8 : q * 8 + 8, place, :] = grad[own, cols].reshape(8, 8, 128)
            for y in range(4):
                srows = pl.ds(pl.multiple_of(owner * 16 + 8 * (y // 2), 8), 8)
                part = small[srows, 128 * (y % 2) : 128 * (y % 2) + 128]
                out[q * 8 + 2 * y, 16:24, :] = part
                out[q * 8 + 2 * y + 1, 16:24, :] = part


def grad_parts(core, activations, out_grads):
    rows, cin = activations.shape
    cout = out_grads.shape[1]
    tile = rows // CHUNKS
    shape = jax.ShapeDtypeStruct((64, 24, 128), F32)
    return pl.pallas_call(
        grad_kernel,
        in_specs=[in_smem(), in_hbm(), in_hbm()],
        out_specs=[in_vmem()] * 2,
        out_shape=[shape, shape],
        scratch_shapes=[
            pltpu.VMEM((rows, cin), F32),
            pltpu.VMEM((rows, cout), F32),
            pltpu.VMEM((2, tile, cin), BF16),
            pltpu.VMEM((2, tile, cin), BF16),
            pltpu.VMEM((2, tile, cout), BF16),
            pltpu.VMEM((2, tile, cout), BF16),
            pltpu.VMEM((cin, cout), F32),
            pltpu.VMEM((cout, cout), F32),
            pltpu.SemaphoreType.DMA((2 * CHUNKS,)),
        ],
        compiler_params=pltpu.CompilerParams(vmem_limit_bytes=56 * 2**20),
        cost_estimate=pl.CostEstimate(flops=6 * rows * (cin + cout) * cout, bytes_accessed=4 * rows * (cin + cout), transcendentals=0),
        name="grad_parts",
    )(core, activations, out_grads)


def stat_kernel(core_ref, a_hbm, mine_ref, other_ref, buf, ah, al, acc, sems):
    cin = acc.shape[0]
    count = cin // 256
    copies = [
        pltpu.make_async_copy(a_hbm.at[:, j * 256 : j * 256 + 256], buf.at[j], sems.at[j]) for j in range(count)
    ]

    def prepare(j):
        if j < count:
            copies[j].wait()
            if j + DEPTH < count:
                copies[j + DEPTH].start()
            cj = slice(j * 256, j * 256 + 256)
            ah[:, cj], al[:, cj] = split(buf[j])

    for copy in copies[:DEPTH]:
        copy.start()
    prepare(0)
    for j in range(count):
        prepare(j + 1)
        cj = slice(j * 256, j * 256 + 256)
        for i in range(j + 1):
            ci = slice(i * 256, i * 256 + 256)
            acc[ci, cj] = gram3(ah[:, ci], al[:, ci], ah[:, cj], al[:, cj])
            if i < j:
                acc[cj, ci] = acc[ci, cj].T
    core = core_ref[0]
    for which, out in ((core, mine_ref), (1 - core, other_ref)):
        for q in range(8):
            own = pl.ds(pl.multiple_of((2 * q + which) * 64, 64), 64)
            for t in range(8):
                part = acc[own, 128 * t : 128 * t + 128]
                out[q * 8 : q * 8 + 8, 8 * t : 8 * t + 8, :] = part.reshape(8, 8, 128)


def stat_parts(core, activations):
    rows, cin = activations.shape
    shape = jax.ShapeDtypeStruct((64, 64, 128), F32)
    return pl.pallas_call(
        stat_kernel,
        in_specs=[in_smem(), in_hbm()],
        out_specs=[in_vmem()] * 2,
        out_shape=[shape, shape],
        scratch_shapes=[
            pltpu.VMEM((cin // 256, rows, 256), F32),
            pltpu.VMEM((rows, cin), BF16),
            pltpu.VMEM((rows, cin), BF16),
            pltpu.VMEM((cin, cin), F32),
            pltpu.SemaphoreType.DMA((cin // 256,)),
        ],
        compiler_params=pltpu.CompilerParams(vmem_limit_bytes=52 * 2**20),
        cost_estimate=pl.CostEstimate(flops=4 * rows * cin * cin, bytes_accessed=4 * rows * cin, transcendentals=0),
        name="stat_parts",
    )(core, activations)


def pack_kernel(mine_ref, got_ref, tail_ref, out_ref):
    lead = mine_ref.shape[1]
    out_ref[:, :lead, :] = mine_ref[...] + got_ref[...]
    for i in range(out_ref.shape[0]):
        out_ref[i, lead:, :] = tail_ref[...]


def pack(mine, got, tail, name):
    chunks, lead, lanes = mine.shape
    extra = tail.shape[0]
    spec = pl.BlockSpec((chunks // 4, lead, lanes), lambda i: (i, 0, 0))
    return pl.pallas_call(
        pack_kernel,
        grid=(4,),
        in_specs=[spec, spec, pl.BlockSpec((extra, lanes), lambda i: (0, 0))],
        out_specs=pl.BlockSpec((chunks // 4, lead + extra, lanes), lambda i: (i, 0, 0)),
        out_shape=jax.ShapeDtypeStruct((chunks, lead + extra, lanes), F32),
        compiler_params=pltpu.CompilerParams(vmem_limit_bytes=16 * 2**20),
        name=name,
    )(mine, got, tail)


def spread_kernel(all_ref, tile_ref, out_ref):
    total = jnp.sum(all_ref[:, :64, :], axis=0)
    for r in range(8):
        out_ref[r, :64, :] = total
        out_ref[r, 64:, :] = tile_ref[...]


def spread(parts, tile):
    return pl.pallas_call(
        spread_kernel,
        out_shape=jax.ShapeDtypeStruct((8, 72, 128), F32),
        compiler_params=pltpu.CompilerParams(vmem_limit_bytes=16 * 2**20),
        name="spread",
    )(parts, tile)


def blend_kernel(rows_ref, fa_ref, fg_ref, na_ref, ng_ref, *, total_rows):
    keep, fresh = decay_rate, 1.0 - decay_rate
    for t in range(8):
        cols = slice(128 * t, 128 * t + 128)
        stat = rows_ref[:, 8 * t : 8 * t + 8, :].reshape(64, 128) / total_rows
        na_ref[:, cols] = keep * fa_ref[:, cols] + fresh * stat
    for y in range(4):
        r, c = slice(8 * (y // 2), 8 * (y // 2) + 8), slice(128 * (y % 2), 128 * (y % 2) + 128)
        ng_ref[r, c] = keep * fg_ref[r, c] + fresh * rows_ref[2 * y, 64:72, :]


def blend(rows, factor_a, factor_g, total_rows):
    return pl.pallas_call(
        lambda *refs: blend_kernel(*refs, total_rows=total_rows),
        out_shape=[jax.ShapeDtypeStruct(factor_a.shape, F32), jax.ShapeDtypeStruct(factor_g.shape, F32)],
        name="blend",
    )(rows, factor_a, factor_g)


def final_kernel(core_ref, inv_a_ref, own_ref, got_ref, inv_own_ref, inv_got_ref, out_ref, grad, inv_g):
    core = core_ref[0]
    for which, part, inv in ((core, own_ref, inv_own_ref), (1 - core, got_ref, inv_got_ref)):
        for q in range(8):
            owner = 2 * q + which
            rows = pl.ds(pl.multiple_of(owner * 64, 64), 64)
            for half in range(2):
                block = part[q * 8 : q * 8 + 8, half * 8 : half * 8 + 8, :]
                grad[rows, half * 128 : half * 128 + 128] = block.reshape(64, 128)
            for y in range(4):
                rows = pl.ds(pl.multiple_of(owner * 16 + 8 * (y // 2), 8), 8)
                inv_g[rows, 128 * (y % 2) : 128 * (y % 2) + 128] = inv[q * 8 + 2 * y]
    high = lax.Precision.HIGHEST
    left = jnp.dot(inv_a_ref[...], grad[...], precision=high, preferred_element_type=F32)
    out_ref[...] = jnp.dot(left, inv_g[...], precision=high, preferred_element_type=F32)


def final(core, inverse_a, own, got, inv_own, inv_got):
    cout = 256
    return pl.pallas_call(
        final_kernel,
        in_specs=[in_smem()] + [in_vmem()] * 5,
        out_specs=in_vmem(),
        out_shape=jax.ShapeDtypeStruct((inverse_a.shape[0], cout), F32),
        scratch_shapes=[pltpu.VMEM((inverse_a.shape[1], cout), F32), pltpu.VMEM((cout, cout), F32)],
        compiler_params=pltpu.CompilerParams(vmem_limit_bytes=16 * 2**20),
        name="final",
    )(core, inverse_a, own, got, inv_own, inv_got)


def twin(flat):
    return (flat // 16) * 16 + (flat + 8) % 16


def swap(array):
    return lax.ppermute(array, SUB, [(i, twin(i)) for i in range(128)])


def exchange(array, axes):
    return lax.all_to_all(array, axes, 0, 0, tiled=True)


def local(activations, out_grads, factor_a, factor_g, inverse_a, inverse_g):
    total_rows = activations.shape[0] * 128
    core = lax.axis_index("co").astype(jnp.int32).reshape(1)
    y = lax.axis_index("y")

    g_mine, g_other = grad_parts(core, activations, out_grads)
    tile = lax.dynamic_slice(inverse_g, (8 * (y // 2), 128 * (y % 2)), (8, 128))
    g_sum = pack(g_mine, swap(g_other), tile, "grad_sum")
    g_sum, core = lax.optimization_barrier((g_sum, core))
    g_all = exchange(g_sum, CHIPS)

    s_mine, s_other = stat_parts(core, activations)
    g_all, s_mine, s_other = lax.optimization_barrier((g_all, s_mine, s_other))
    g_own = jnp.sum(g_all[:, :24], axis=0)
    inv_own = g_all[:, 24:]
    s_sum = pack(s_mine, swap(s_other), g_own[:16], "stat_sum")
    s_all = exchange(s_sum, CHIPS)
    inv_got = swap(inv_own)

    own = s_all[:, 64:]
    got = swap(own)
    rows = exchange(spread(s_all, g_own[16:]), ("y", "zh"))
    precond_grad = final(core, inverse_a, own, got, inv_own, inv_got)
    rows, precond_grad = lax.optimization_barrier((rows, precond_grad))
    new_factor_a, new_factor_g = blend(rows, factor_a, factor_g, total_rows)
    return new_factor_a, new_factor_g, precond_grad


def solution(mesh):
    fine = jax.sharding.Mesh(mesh.devices.reshape(SIZES), SUB)
    rows = P(SUB, None)
    panel = P(("x", "zl", "co"), None)
    return jax.shard_map(
        local,
        mesh=fine,
        in_specs=(rows, rows, panel, panel, panel, panel),
        out_specs=(panel, panel, panel),
        check_vma=False,
    )
```

time: 142 us -> 122 us (0.86)
  blocking collectives: 0 us -> 45 us
  starting transfers between devices: 53.4 us -> 18.8 us
  waiting for transfers between devices: 29.8 us -> 11.6 us
  between operations: 14.2 us -> 0.73 us
  Pallas kernels: 33.2 us -> 41.4 us
  other arithmetic: 8.2 us -> 0.08 us
    all_to_all x0 -> x1, blocking collectives: none -> 45 us  [exchange(): return lax.all_to_all(array, axes, 0, 0, tiled=True)]
    ppermute x9 -> x4, starting transfers between devices: 27.6 us -> 4.03 us  [swap(): return lax.ppermute(array, SUB, [(i, twin(i)) for i in range(128)])]
    ppermute x9 -> x4, waiting for transfers between devices: 23.8 us -> 5.35 us  [swap(): return lax.ppermute(array, SUB, [(i, twin(i)) for i in range(128)])]
    all_to_all x3 -> x2, starting transfers between devices: 25.5 us -> 14.8 us  [exchange(): return lax.all_to_all(array, axes, 0, 0, tiled=True)]
    pallas_call x3 -> x7, Pallas kernels: 33.2 us -> 41.4 us  [the longest x1 21.2 us: stat_parts(): pl.pallas_call(stat_kernel, in_specs=[in_smem(), in_hbm()], out_specs=[in...]
    add x3 -> x0, other arithmetic: 3.45 us -> none  [the longest x1 2.1 us: local(): g_sum = g_mine + move(g_other, CORE)]
    reshape x1 -> x0, other arithmetic: 3.29 us -> none  [local(): s_all = lax.all_to_all(s_sum.reshape(64, 8, 1024), CHIPS, 0, 0, tiled=True)]
    unnamed x10 -> x8, local copies, waits for them, and re-layouts: 0.71 us -> 3.45 us
  transfers between devices with their start and end apart: 13 -> 6, of which waited for: 7 -> 3; matrix products, arithmetic and copies ran while one was open for 5% -> 1% of each run, Pallas kernels for 15% -> 20%
where the time goes in v3:
time: 122 us
  blocking collectives  45 us (37%)
  Pallas kernels  41.4 us (34%)
  starting transfers between devices  18.8 us (15%)
  waiting for transfers between devices  11.6 us (10%)
  local copies, waits for them, and re-layouts  4.21 us (3%)
    all_to_all x1, blocking collectives, exchange(): return lax.all_to_all(array, axes, 0, 0, tiled=True)  45 us
    pallas_call x1, Pallas kernels, stat_parts(): pl.pallas_call(stat_kernel, in_specs=[in_smem(), in_hbm()], out_specs=[in...  21.2 us
    all_to_all x2, starting transfers between devices, exchange(): return lax.all_to_all(array, axes, 0, 0, tiled=True)  14.8 us
    pallas_call x1, Pallas kernels, grad_parts(): pl.pallas_call(grad_kernel, in_specs=[in_smem(), in_hbm(), in_hbm()], out...  13.9 us
    all_to_all x2, waiting for transfers between devices, exchange(): return lax.all_to_all(array, axes, 0, 0, tiled=True)  6.3 us
    ppermute x4, waiting for transfers between devices, swap(): return lax.ppermute(array, SUB, [(i, twin(i)) for i in range(128)])  5.35 us
    ppermute x4, starting transfers between devices, swap(): return lax.ppermute(array, SUB, [(i, twin(i)) for i in range(128)])  4.03 us
    unnamed x8, local copies, waits for them, and re-layouts  3.45 us
  transfers between devices with their start and end apart: 6, of which 3 were waited for; matrix products, arithmetic and copies ran while one was open for 1% of the time, Pallas kernels for 20%

profile of v3, /device:TPU:1, one launch (start us, length us, event | category | flops | bytes accessed | tf_op | source)
XLA Modules:
  0.0 121.9 jit_solution(16134702535586754759)
XLA Ops:
  0.6 13.9 %grad_parts.1 = (f32[64,24,128]{2,1,0:T(8,128)}, f32[64,24,128]{2,1,0:T(8,128)}) custom-call(s32[1]{0:T(128)} %bitcast.core_ref, f32[3072,1024]{1,0:T(8,128)} %a_hbm.3, f32[3072,256]{1,0:T(8,128)} %g_hbm.1), custom_call_target="tpu_custom_call" | custom-call | flops 6039797760 | bytes 15728640 | tf_op jit(solution)/shard_map/grad_parts/pallas_call | solution.py:104
  14.6 1.5 %collective-permute-start = (f32[64,24,128]{2,1,0:T(8,128)}, f32[64,24,128]{2,1,0:T(8,128)S(1)}, u32[]{:S(2)}, u32[]{:S(2)}) collective-permute-start(f32[64,24,128]{2,1,0:T(8,128)} %get-tuple-element.17), channel_id=1, source_target_pairs={{0,8},{1,9},{2,10},{3,11},{4,12},{5,13},{6,14},{7,15},{8,0},{9,1},... | collective-permute-start | bytes 2359304 | tf_op jit(solution)/shard_map/ppermute | solution.py:274
  16.1 0.7 dynamic_slice.3.tail_ref
  16.8 1.4 %collective-permute-done.got_ref = f32[64,24,128]{2,1,0:T(8,128)S(1)} collective-permute-done((f32[64,24,128]{2,1,0:T(8,128)}, f32[64,24,128]{2,1,0:T(8,128)S(1)}, u32[]{:S(2)}, u32[]{:S(2)}) %collective-permute-start) | collective-permute-done | bytes 786464 | tf_op jit(solution)/shard_map/ppermute | solution.py:274
  18.2 1.1 copy-done.1
  19.3 1.5 %grad_sum.1 = f32[64,32,128]{2,1,0:T(8,128)} custom-call(f32[64,24,128]{2,1,0:T(8,128)S(1)} %copy-done.1, f32[64,24,128]{2,1,0:T(8,128)S(1)} %collective-permute-done.got_ref, f32[8,128]{1,0:T(8,128)S(1)} %dynamic_slice.3.tail_ref), custom_call_target="tpu_custom_call" | custom-call | tf_op jit(solution)/shard_map/grad_sum/pallas_call | solution.py:193
  20.9 11.4 %all-to-all-start = ((f32[64,32,128]{2,1,0:T(8,128)}), f32[64,32,128]{2,1,0:T(8,128)S(1)}, u32[]{:S(2)}, u32[]{:S(2)}) async-start(f32[64,32,128]{2,1,0:T(8,128)} %grad_sum.1), calls=%async_computation | async-start | bytes 2097152 | tf_op jit(solution)/shard_map/all_to_all | solution.py:278
  32.3 21.2 %stat_parts.1 = (f32[64,64,128]{2,1,0:T(8,128)}, f32[64,64,128]{2,1,0:T(8,128)}) custom-call(s32[1]{0:T(128)} %bitcast.core_ref, f32[3072,1024]{1,0:T(8,128)} %a_hbm.3), custom_call_target="tpu_custom_call" | custom-call | flops 12884901888 | bytes 12582912 | tf_op jit(solution)/shard_map/stat_parts/pallas_call | solution.py:164
  53.5 0.0 all-to-all-done
  53.5 0.7 collective-permute-start.1
  54.3 0.1 slice_reduce_fusion
  54.4 3.9 %collective-permute-done.1.got_ref = f32[64,64,128]{2,1,0:T(8,128)S(1)} collective-permute-done((f32[64,64,128]{2,1,0:T(8,128)}, f32[64,64,128]{2,1,0:T(8,128)S(1)}, u32[]{:S(2)}, u32[]{:S(2)}) %collective-permute-start.1) | collective-permute-done | bytes 2097184 | tf_op jit(solution)/shard_map/ppermute | solution.py:274
  58.3 1.6 %copy-done = f32[64,64,128]{2,1,0:T(8,128)S(1)} copy-done((f32[64,64,128]{2,1,0:T(8,128)S(1)}, f32[64,64,128]{2,1,0:T(8,128)}, u32[]{:S(2)}) %copy-start) | copy-done | bytes 2097176
  59.9 0.3 stat_sum.1
  60.1 45.0 %all_to_all.15.all_ref = f32[64,80,128]{2,1,0:T(8,128)S(1)} all-to-all(f32[64,80,128]{2,1,0:T(8,128)S(1)} %stat_sum.1), channel_id=1, replica_groups=mesh['x'=4,'zl'=2,'co'=2,'y'=4,'zh'=2] {'x','zl','y','zh'}, dimensions={0} | all-to-all | bytes 5242880 | tf_op jit(solution)/shard_map/all_to_all | solution.py:278
  105.2 1.7 %collective-permute-start.2 = (f32[64,16,128]{2,1,0:T(8,128)S(1)}, f32[64,16,128]{2,1,0:T(8,128)S(1)}, u32[]{:S(2)}, u32[]{:S(2)}) collective-permute-start(f32[64,16,128]{2,1,0:T(8,128)S(1)} %slice.22.own_ref), channel_id=1, source_target_pairs={{0,8},{1,9},{2,10},{3,11},{4,12},{5,13},{6,14},{7,15},{8,0},{9,1},... | collective-permute-start | bytes 1572872 | tf_op jit(solution)/shard_map/ppermute | solution.py:274
  106.9 0.1 collective-permute-start.3
  107.0 0.9 spread.1
  107.9 3.4 %all-to-all-start.2 = ((f32[8,72,128]{2,1,0:T(8,128)}), f32[8,72,128]{2,1,0:T(8,128)S(1)}, u32[]{:S(2)}, u32[]{:S(2)}) async-start(f32[8,72,128]{2,1,0:T(8,128)} %spread.1), calls=%async_computation.2 | async-start | bytes 589824 | tf_op jit(solution)/shard_map/all_to_all | solution.py:278
  111.3 0.0 collective-permute-done.3.inv_got_ref
  111.3 1.8 %final.1 = f32[64,256]{1,0:T(8,128)} custom-call(s32[1]{0:T(128)} %bitcast.core_ref, f32[64,1024]{1,0:T(8,128)S(1)} %copy-done.2, f32[64,16,128]{2,1,0:T(8,128)S(1)} %slice.22.own_ref, f32[64,16,128]{2,1,0:T(8,128)S(1)} %collective-permute-done.2.got_ref, f32[64,8,128]{2,1,0:T(8,128)S(1)} %slice.19.inv_own_ref, ...), custom_call_target="tpu_custom_call" | custom-call | tf_op jit(solution)/shard_map/final/pallas_call | solution.py:258
  113.1 6.3 %all-to-all-done.2.refs_0_ = f32[8,72,128]{2,1,0:T(8,128)S(1)} async-done(((f32[8,72,128]{2,1,0:T(8,128)}), f32[8,72,128]{2,1,0:T(8,128)S(1)}, u32[]{:S(2)}, u32[]{:S(2)}) %all-to-all-start.2) | async-done | bytes 294944 | tf_op jit(solution)/shard_map/all_to_all | solution.py:278
  119.4 0.7 copy-done.3
  120.1 1.8 %blend.1 = (f32[64,1024]{1,0:T(8,128)}, f32[16,256]{1,0:T(8,128)}) custom-call(f32[8,72,128]{2,1,0:T(8,128)} %copy-done.3, f32[64,1024]{1,0:T(8,128)} %refs_1_.1, f32[16,256]{1,0:T(8,128)} %refs_2_.1), custom_call_target="tpu_custom_call" | custom-call | tf_op jit(solution)/shard_map/blend/pallas_call | solution.py:232
  (10 shorter events, 0.1 us)
Async XLA Ops:
  14.6 3.6 %collective-permute-start = (f32[64,24,128]{2,1,0:T(8,128)}, f32[64,24,128]{2,1,0:T(8,128)S(1)}, u32[]{:S(2)}, u32[]{:S(2)}) collective-permute-start(f32[64,24,128]{2,1,0:T(8,128)} %get-tuple-element.17), channel_id=1, source_target_pairs={{0,8},{1,9},{2,10},{3,11},{4,12},{5,13},{6,14},{7,15},{8,0},{9,1},... | collective-permute-start | bytes 2359304 | tf_op jit(solution)/shard_map/ppermute | solution.py:274
  18.2 1.1 copy-start.1
  20.9 32.6 %all-to-all-start = ((f32[64,32,128]{2,1,0:T(8,128)}), f32[64,32,128]{2,1,0:T(8,128)S(1)}, u32[]{:S(2)}, u32[]{:S(2)}) async-start(f32[64,32,128]{2,1,0:T(8,128)} %grad_sum.1), calls=%async_computation | async-start | bytes 2097152 | tf_op jit(solution)/shard_map/all_to_all | solution.py:278
  53.5 4.7 %collective-permute-start.1 = (f32[64,64,128]{2,1,0:T(8,128)}, f32[64,64,128]{2,1,0:T(8,128)S(1)}, u32[]{:S(2)}, u32[]{:S(2)}) collective-permute-start(f32[64,64,128]{2,1,0:T(8,128)} %get-tuple-element.23), channel_id=1, source_target_pairs={{0,8},{1,9},{2,10},{3,11},{4,12},{5,13},{6,14},{7,15},{8,0},{9,1},... | collective-permute-start | bytes 6291464 | tf_op jit(solution)/shard_map/ppermute | solution.py:274
  58.3 1.6 %copy-start = (f32[64,64,128]{2,1,0:T(8,128)S(1)}, f32[64,64,128]{2,1,0:T(8,128)}, u32[]{:S(2)}) copy-start(f32[64,64,128]{2,1,0:T(8,128)} %get-tuple-element.22.mine_ref) | copy-start | bytes 6291460
  105.1 6.2 %copy-start.2 = (f32[64,1024]{1,0:T(8,128)S(1)}, f32[64,1024]{1,0:T(8,128)}, u32[]{:S(2)}) copy-start(f32[64,1024]{1,0:T(8,128)} %inv_a_ref.1) | copy-start | bytes 786436
  105.2 6.1 %collective-permute-start.2 = (f32[64,16,128]{2,1,0:T(8,128)S(1)}, f32[64,16,128]{2,1,0:T(8,128)S(1)}, u32[]{:S(2)}, u32[]{:S(2)}) collective-permute-start(f32[64,16,128]{2,1,0:T(8,128)S(1)} %slice.22.own_ref), channel_id=1, source_target_pairs={{0,8},{1,9},{2,10},{3,11},{4,12},{5,13},{6,14},{7,15},{8,0},{9,1},... | collective-permute-start | bytes 1572872 | tf_op jit(solution)/shard_map/ppermute | solution.py:274
  106.9 4.4 %collective-permute-start.3 = (f32[64,8,128]{2,1,0:T(8,128)S(1)}, f32[64,8,128]{2,1,0:T(8,128)S(1)}, u32[]{:S(2)}, u32[]{:S(2)}) collective-permute-start(f32[64,8,128]{2,1,0:T(8,128)S(1)} %slice.19.inv_own_ref), channel_id=1, source_target_pairs={{0,8},{1,9},{2,10},{3,11},{4,12},{5,13},{6,14},{7,15},{8,0},{9,1},... | collective-permute-start | bytes 786440 | tf_op jit(solution)/shard_map/ppermute | solution.py:274
  107.9 11.5 %all-to-all-start.2 = ((f32[8,72,128]{2,1,0:T(8,128)}), f32[8,72,128]{2,1,0:T(8,128)S(1)}, u32[]{:S(2)}, u32[]{:S(2)}) async-start(f32[8,72,128]{2,1,0:T(8,128)} %spread.1), calls=%async_computation.2 | async-start | bytes 589824 | tf_op jit(solution)/shard_map/all_to_all | solution.py:278
  119.4 0.7 copy-start.3

commit v4 on v3

--- a/solution.py
+++ b/solution.py
@@ -40,7 +40,7 @@
     return pl.BlockSpec(memory_space=pltpu.SMEM)
 
 
-def grad_kernel(core_ref, a_hbm, g_hbm, mine_ref, other_ref, abuf, gbuf, ah, al, gh, gl, grad, small, sems):
+def grad_kernel(core_ref, a_hbm, g_hbm, mine_ref, other_ref, abuf, gbuf, grad, small, sems):
     rows, cin = abuf.shape
     tile = rows // CHUNKS
     copies = []
@@ -53,31 +53,23 @@
             )
         )
 
-    def fetch(k):
-        if k < CHUNKS:
-            for copy in copies[k]:
+    for k in range(DEPTH):
+        for copy in copies[k]:
+            copy.start()
+    for k in range(CHUNKS):
+        for copy in copies[k]:
+            copy.wait()
+        if k + DEPTH < CHUNKS:
+            for copy in copies[k + DEPTH]:
                 copy.start()
-
-    def prepare(k):
-        if k < CHUNKS:
-            for copy in copies[k]:
-                copy.wait()
-            fetch(k + DEPTH)
-            r = slice(k * tile, k * tile + tile)
-            gh[k % 2], gl[k % 2] = split(gbuf[r, :])
-            ah[k % 2], al[k % 2] = split(abuf[r, :])
-
-    for k in range(DEPTH):
-        fetch(k)
-    prepare(0)
-    for k in range(CHUNKS):
-        prepare(k + 1)
-        now = k % 2
+        r = slice(k * tile, k * tile + tile)
+        gh, gl = split(gbuf[r, :])
+        ah, al = split(abuf[r, :])
         for j in range(0, cin, 256):
             c = slice(j, j + 256)
-            part = gram3(ah[now, :, c], al[now, :, c], gh[now], gl[now])
+            part = gram3(ah[:, c], al[:, c], gh, gl)
             grad[c, :] = part if k == 0 else grad[c, :] + part
-        part = gram3(gh[now], gl[now], gh[now], gl[now])
+        part = gram3(gh, gl, gh, gl)
         small[...] = part if k == 0 else small[...] + part
 
     core = core_ref[0]
@@ -99,7 +91,6 @@
 def grad_parts(core, activations, out_grads):
     rows, cin = activations.shape
     cout = out_grads.shape[1]
-    tile = rows // CHUNKS
     shape = jax.ShapeDtypeStruct((64, 24, 128), F32)
     return pl.pallas_call(
         grad_kernel,
@@ -109,10 +100,6 @@
         scratch_shapes=[
             pltpu.VMEM((rows, cin), F32),
             pltpu.VMEM((rows, cout), F32),
-            pltpu.VMEM((2, tile, cin), BF16),
-            pltpu.VMEM((2, tile, cin), BF16),
-            pltpu.VMEM((2, tile, cout), BF16),
-            pltpu.VMEM((2, tile, cout), BF16),
             pltpu.VMEM((cin, cout), F32),
             pltpu.VMEM((cout, cout), F32),
             pltpu.SemaphoreType.DMA((2 * CHUNKS,)),
@@ -130,37 +117,44 @@
         pltpu.make_async_copy(a_hbm.at[:, j * 256 : j * 256 + 256], buf.at[j], sems.at[j]) for j in range(count)
     ]
 
-    def prepare(j):
-        if j < count:
-            copies[j].wait()
-            if j + DEPTH < count:
-                copies[j + DEPTH].start()
-            cj = slice(j * 256, j * 256 + 256)
-            ah[:, cj], al[:, cj] = split(buf[j])
-
     for copy in copies[:DEPTH]:
         copy.start()
-    prepare(0)
     for j in range(count):
-        prepare(j + 1)
+        copies[j].wait()
+        if j + DEPTH < count:
+            copies[j + DEPTH].start()
         cj = slice(j * 256, j * 256 + 256)
+        ah[:, cj], al[:, cj] = split(buf[j])
         for i in range(j + 1):
             ci = slice(i * 256, i * 256 + 256)
             acc[ci, cj] = gram3(ah[:, ci], al[:, ci], ah[:, cj], al[:, cj])
             if i < j:
                 acc[cj, ci] = acc[ci, cj].T
-    core = core_ref[0]
-    for which, out in ((core, mine_ref), (1 - core, other_ref)):
-        for q in range(8):
-            own = pl.ds(pl.multiple_of((2 * q + which) * 64, 64), 64)
-            for t in range(8):
-                part = acc[own, 128 * t : 128 * t + 128]
-                out[q * 8 : q * 8 + 8, 8 * t : 8 * t + 8, :] = part.reshape(8, 8, 128)
+
+    low = lax.broadcasted_iota(jnp.int32, (32, 128), 1) < 64
+    for side in range(2):
+
+        @pl.when(core_ref[0] == side)
+        def _():
+            for p in range(16):
+                out = mine_ref if p % 2 == side else other_ref
+                for r in range(8):
+                    place = p // 2 * 8 + r
+                    c = (p + r) % 16
+                    block = acc[64 * p : 64 * p + 64, c // 2 * 128 : c // 2 * 128 + 128]
+                    top, bottom = block[:32], block[32:]
+                    if c % 2 == 0:
+                        bottom = pltpu.roll(bottom, 64, 1)
+                    else:
+                        top = pltpu.roll(top, 64, 1)
+                    out[place, :32, :] = jnp.where(low, top, bottom)
+                    far = (p + 8) % 16 // 2 * 128
+                    out[place, 32:, :] = acc[64 * p + 8 * r : 64 * p + 8 * r + 8, far : far + 128]
 
 
 def stat_parts(core, activations):
     rows, cin = activations.shape
-    shape = jax.ShapeDtypeStruct((64, 64, 128), F32)
+    shape = jax.ShapeDtypeStruct((64, 40, 128), F32)
     return pl.pallas_call(
         stat_kernel,
         in_specs=[in_smem(), in_hbm()],
@@ -201,39 +195,61 @@
     )(mine, got, tail)
 
 
-def spread_kernel(all_ref, tile_ref, out_ref):
-    total = jnp.sum(all_ref[:, :64, :], axis=0)
+def spread_kernel(near_ref, mirror_ref, tile_ref, out_ref):
     for r in range(8):
-        out_ref[r, :64, :] = total
-        out_ref[r, 64:, :] = tile_ref[...]
-
-
-def spread(parts, tile):
+        out_ref[r, :32, :] = near_ref[:32, :]
+        out_ref[r, 32:64, :] = mirror_ref[...]
+        out_ref[r, 64:72, :] = near_ref[32:40, :]
+        out_ref[r, 72:, :] = tile_ref[...]
+
+
+def spread(near, mirror, tile):
     return pl.pallas_call(
         spread_kernel,
-        out_shape=jax.ShapeDtypeStruct((8, 72, 128), F32),
-        compiler_params=pltpu.CompilerParams(vmem_limit_bytes=16 * 2**20),
+        out_shape=jax.ShapeDtypeStruct((8, 80, 128), F32),
         name="spread",
-    )(parts, tile)
-
-
-def blend_kernel(rows_ref, fa_ref, fg_ref, na_ref, ng_ref, *, total_rows):
+    )(near, mirror, tile)
+
+
+def blend_kernel(place_ref, rows_ref, fa_ref, fg_ref, na_ref, ng_ref, stat, *, total_rows):
     keep, fresh = decay_rate, 1.0 - decay_rate
-    for t in range(8):
-        cols = slice(128 * t, 128 * t + 128)
-        stat = rows_ref[:, 8 * t : 8 * t + 8, :].reshape(64, 128) / total_rows
-        na_ref[:, cols] = keep * fa_ref[:, cols] + fresh * stat
+    panel = place_ref[1]
+    for c in range(16):
+        cols = slice(64 * c, 64 * c + 64)
+        k = (c - panel + 16) % 16
+
+        @pl.when(k < 8)
+        def _():
+            block = rows_ref[k, :32, :]
+            stat[:32, cols] = block[:, :64]
+            stat[32:, cols] = block[:, 64:]
+
+        @pl.when(k == 8)
+        def _():
+            half = 64 * (c % 2)
+            stat[:, cols] = rows_ref[:, 64:72, :].reshape(64, 128)[:, half : half + 64]
+
+        @pl.when(k > 8)
+        def _():
+            turned = rows_ref[16 - k, 32:64, :].T
+            stat[:, 64 * c : 64 * c + 32] = turned[:64]
+            stat[:, 64 * c + 32 : 64 * c + 64] = turned[64:]
+
+    na_ref[...] = keep * fa_ref[...] + fresh * (stat[...] / total_rows)
     for y in range(4):
         r, c = slice(8 * (y // 2), 8 * (y // 2) + 8), slice(128 * (y % 2), 128 * (y % 2) + 128)
-        ng_ref[r, c] = keep * fg_ref[r, c] + fresh * rows_ref[2 * y, 64:72, :]
-
-
-def blend(rows, factor_a, factor_g, total_rows):
+        ng_ref[r, c] = keep * fg_ref[r, c] + fresh * rows_ref[2 * y, 72:80, :]
+
+
+def blend(place, rows, factor_a, factor_g, total_rows):
     return pl.pallas_call(
         lambda *refs: blend_kernel(*refs, total_rows=total_rows),
+        in_specs=[in_smem()] + [in_vmem()] * 3,
+        out_specs=[in_vmem()] * 2,
         out_shape=[jax.ShapeDtypeStruct(factor_a.shape, F32), jax.ShapeDtypeStruct(factor_g.shape, F32)],
+        scratch_shapes=[pltpu.VMEM(factor_a.shape, F32)],
         name="blend",
-    )(rows, factor_a, factor_g)
+    )(place, rows, factor_a, factor_g)
 
 
 def final_kernel(core_ref, inv_a_ref, own_ref, got_ref, inv_own_ref, inv_got_ref, out_ref, grad, inv_g):
@@ -270,8 +286,13 @@
     return (flat // 16) * 16 + (flat + 8) % 16
 
 
-def swap(array):
-    return lax.ppermute(array, SUB, [(i, twin(i)) for i in range(128)])
+def across(flat):
+    panel, rep = flat // 8, flat % 8
+    return (panel + rep) % 16 * 8 + rep
+
+
+def swap(array, to=twin):
+    return lax.ppermute(array, SUB, [(i, to(i)) for i in range(128)])
 
 
 def exchange(array, axes):
@@ -280,7 +301,7 @@
 
 def local(activations, out_grads, factor_a, factor_g, inverse_a, inverse_g):
     total_rows = activations.shape[0] * 128
-    core = lax.axis_index("co").astype(jnp.int32).reshape(1)
+    core = jnp.stack([lax.axis_index("co"), lax.axis_index(("x", "zl", "co"))]).astype(jnp.int32)
     y = lax.axis_index("y")
 
     g_mine, g_other = grad_parts(core, activations, out_grads)
@@ -297,12 +318,14 @@
     s_all = exchange(s_sum, CHIPS)
     inv_got = swap(inv_own)
 
-    own = s_all[:, 64:]
+    near = jnp.sum(s_all[:, :40], axis=0)
+    mirror = swap(near[:32], across)
+    own = s_all[:, 40:]
     got = swap(own)
-    rows = exchange(spread(s_all, g_own[16:]), ("y", "zh"))
+    rows = exchange(spread(near, mirror, g_own[16:]), ("y", "zh"))
     precond_grad = final(core, inverse_a, own, got, inv_own, inv_got)
     rows, precond_grad = lax.optimization_barrier((rows, precond_grad))
-    new_factor_a, new_factor_g = blend(rows, factor_a, factor_g, total_rows)
+    new_factor_a, new_factor_g = blend(core, rows, factor_a, factor_g, total_rows)
     return new_factor_a, new_factor_g, precond_grad
 
 

time: 122 us -> 118 us (0.967)
  blocking collectives: 45 us -> 35.9 us
  starting transfers between devices: 18.8 us -> 25.7 us
  waiting for transfers between devices: 11.6 us -> 8.27 us
    all_to_all x1, blocking collectives: 45 us -> 35.9 us  [exchange(): return lax.all_to_all(array, axes, 0, 0, tiled=True)]
    all_to_all x2, starting transfers between devices: 14.8 us -> 19.6 us  [exchange(): return lax.all_to_all(array, axes, 0, 0, tiled=True)]
    all_to_all x2, waiting for transfers between devices: 6.3 us -> 2.88 us  [exchange(): return lax.all_to_all(array, axes, 0, 0, tiled=True)]
    ppermute x4 -> x5, starting transfers between devices: 4.03 us -> 6.13 us  [swap(): return lax.ppermute(array, SUB, [(i, to(i)) for i in range(128)])]
    pallas_call x1, Pallas kernels: 1.8 us -> 3.6 us  [blend(): pl.pallas_call(lambda *refs: blend_kernel(*refs, total_rows=total_rows),...]
    pallas_call x1, Pallas kernels: 21.2 us -> 19.8 us  [stat_parts(): pl.pallas_call(stat_kernel, in_specs=[in_smem(), in_hbm()], out_specs=[in...]
    pallas_call x1, Pallas kernels: 13.9 us -> 12.5 us  [grad_parts(): pl.pallas_call(grad_kernel, in_specs=[in_smem(), in_hbm(), in_hbm()], out...]
    unnamed x8 -> x12, local copies, waits for them, and re-layouts: 3.45 us -> 2.47 us
  transfers between devices with their start and end apart: 6 -> 7, of which waited for: 3 -> 4; matrix products, arithmetic and copies ran while one was open for 1% -> 1% of each run, Pallas kernels for 20% -> 20%
where the time goes in v4:
time: 118 us; the launch traced here: 117 us
  Pallas kernels  41.5 us (35%)
  blocking collectives  35.9 us (30%)
  starting transfers between devices  25.7 us (22%)
  waiting for transfers between devices  8.27 us (7%)
  local copies, waits for them, and re-layouts  3.83 us (3%)
    all_to_all x1, blocking collectives, exchange(): return lax.all_to_all(array, axes, 0, 0, tiled=True)  35.9 us
    pallas_call x1, Pallas kernels, stat_parts(): pl.pallas_call(stat_kernel, in_specs=[in_smem(), in_hbm()], out_specs=[in...  19.8 us
    all_to_all x2, starting transfers between devices, exchange(): return lax.all_to_all(array, axes, 0, 0, tiled=True)  19.6 us
    pallas_call x1, Pallas kernels, grad_parts(): pl.pallas_call(grad_kernel, in_specs=[in_smem(), in_hbm(), in_hbm()], out...  12.5 us
    ppermute x5, starting transfers between devices, swap(): return lax.ppermute(array, SUB, [(i, to(i)) for i in range(128)])  6.13 us
    ppermute x5, waiting for transfers between devices, swap(): return lax.ppermute(array, SUB, [(i, to(i)) for i in range(128)])  5.39 us
    pallas_call x1, Pallas kernels, blend(): pl.pallas_call(lambda *refs: blend_kernel(*refs, total_rows=total_rows),...  3.6 us
    all_to_all x2, waiting for transfers between devices, exchange(): return lax.all_to_all(array, axes, 0, 0, tiled=True)  2.88 us
  transfers between devices with their start and end apart: 7, of which 4 were waited for; matrix products, arithmetic and copies ran while one was open for 1% of the time, Pallas kernels for 20%

profile of v4, /device:TPU:1, one launch (start us, length us, event | category | flops | bytes accessed | tf_op | source)
XLA Modules:
  0.0 116.7 jit_solution(8239540815894568249)
XLA Ops:
  0.6 0.6 pad_add_fusion.core_ref.refs_0_
  1.2 12.5 %grad_parts.1 = (f32[64,24,128]{2,1,0:T(8,128)}, f32[64,24,128]{2,1,0:T(8,128)}) custom-call(s32[2]{0:T(128)} %pad_add_fusion.core_ref.refs_0_, f32[3072,1024]{1,0:T(8,128)} %a_hbm.3, f32[3072,256]{1,0:T(8,128)} %g_hbm.1), custom_call_target="tpu_custom_call" | custom-call | flops 6039797760 | bytes 15728640 | tf_op jit(solution)/shard_map/grad_parts/pallas_call | solution.py:95
  13.8 1.5 %collective-permute-start = (f32[64,24,128]{2,1,0:T(8,128)}, f32[64,24,128]{2,1,0:T(8,128)S(1)}, u32[]{:S(2)}, u32[]{:S(2)}) collective-permute-start(f32[64,24,128]{2,1,0:T(8,128)} %get-tuple-element.17), channel_id=1, source_target_pairs={{0,8},{1,9},{2,10},{3,11},{4,12},{5,13},{6,14},{7,15},{8,0},{9,1},... | collective-permute-start | bytes 2359304 | tf_op jit(solution)/shard_map/ppermute | solution.py:295
  15.3 0.7 dynamic_slice.3.tail_ref
  16.0 1.4 %collective-permute-done.got_ref = f32[64,24,128]{2,1,0:T(8,128)S(1)} collective-permute-done((f32[64,24,128]{2,1,0:T(8,128)}, f32[64,24,128]{2,1,0:T(8,128)S(1)}, u32[]{:S(2)}, u32[]{:S(2)}) %collective-permute-start) | collective-permute-done | bytes 786464 | tf_op jit(solution)/shard_map/ppermute | solution.py:295
  17.4 1.1 copy-done
  18.5 1.5 %grad_sum.1 = f32[64,32,128]{2,1,0:T(8,128)} custom-call(f32[64,24,128]{2,1,0:T(8,128)S(1)} %copy-done, f32[64,24,128]{2,1,0:T(8,128)S(1)} %collective-permute-done.got_ref, f32[8,128]{1,0:T(8,128)S(1)} %dynamic_slice.3.tail_ref), custom_call_target="tpu_custom_call" | custom-call | tf_op jit(solution)/shard_map/grad_sum/pallas_call | solution.py:187
  20.1 11.4 %all-to-all-start = ((f32[64,32,128]{2,1,0:T(8,128)}), f32[64,32,128]{2,1,0:T(8,128)S(1)}, u32[]{:S(2)}, u32[]{:S(2)}) async-start(f32[64,32,128]{2,1,0:T(8,128)} %grad_sum.1), calls=%async_computation | async-start | bytes 2097152 | tf_op jit(solution)/shard_map/all_to_all | solution.py:299
  31.5 19.8 %stat_parts.1 = (f32[64,40,128]{2,1,0:T(8,128)S(1)}, f32[64,40,128]{2,1,0:T(8,128)}) custom-call(s32[2]{0:T(128)S(1)} %copy-done.2, f32[3072,1024]{1,0:T(8,128)} %a_hbm.3), custom_call_target="tpu_custom_call" | custom-call | flops 12884901888 | bytes 12582912 | tf_op jit(solution)/shard_map/stat_parts/pallas_call | solution.py:158
  51.3 0.7 collective-permute-start.1
  52.2 2.8 %collective-permute-done.1.got_ref = f32[64,40,128]{2,1,0:T(8,128)S(1)} collective-permute-done((f32[64,40,128]{2,1,0:T(8,128)}, f32[64,40,128]{2,1,0:T(8,128)S(1)}, u32[]{:S(2)}, u32[]{:S(2)}) %collective-permute-start.1) | collective-permute-done | bytes 1310752 | tf_op jit(solution)/shard_map/ppermute | solution.py:295
  55.2 35.9 %all_to_all.15 = f32[64,56,128]{2,1,0:T(8,128)S(1)} all-to-all(f32[64,56,128]{2,1,0:T(8,128)S(1)} %stat_sum.1), channel_id=1, replica_groups=mesh['x'=4,'zl'=2,'co'=2,'y'=4,'zh'=2] {'x','zl','y','zh'}, dimensions={0} | all-to-all | bytes 3670016 | tf_op jit(solution)/shard_map/all_to_all | solution.py:299
  91.1 2.1 %collective-permute-start.3 = (f32[64,16,128]{2,1,0:T(8,128)S(1)}, f32[64,16,128]{2,1,0:T(8,128)S(1)}, u32[]{:S(2)}, u32[]{:S(2)}) collective-permute-start(f32[64,16,128]{2,1,0:T(8,128)S(1)} %slice.32.own_ref), channel_id=1, source_target_pairs={{0,8},{1,9},{2,10},{3,11},{4,12},{5,13},{6,14},{7,15},{8,0},{9,1},... | collective-permute-start | bytes 1572872 | tf_op jit(solution)/shard_map/ppermute | solution.py:295
  93.3 0.7 collective-permute-start.2
  93.9 0.6 slice.31.tile_ref
  94.5 0.6 copy-done.5
  95.2 1.5 %spread.1 = f32[8,80,128]{2,1,0:T(8,128)} custom-call(f32[40,128]{1,0:T(8,128)} %copy-done.4, f32[32,128]{1,0:T(8,128)} %copy-done.5, f32[8,128]{1,0:T(8,128)} %slice.31.tile_ref), custom_call_target="tpu_custom_call" | custom-call | tf_op jit(solution)/shard_map/spread/pallas_call | solution.py:207
  96.6 8.2 %all-to-all-start.2 = ((f32[8,80,128]{2,1,0:T(8,128)}), f32[8,80,128]{2,1,0:T(8,128)S(1)}, u32[]{:S(2)}, u32[]{:S(2)}) async-start(f32[8,80,128]{2,1,0:T(8,128)} %spread.1), calls=%async_computation.2 | async-start | bytes 655360 | tf_op jit(solution)/shard_map/all_to_all | solution.py:299
  104.9 1.1 collective-permute-start.4
  106.0 1.2 collective-permute-done.4.inv_got_ref
  107.2 2.3 %final.1 = f32[64,256]{1,0:T(8,128)} custom-call(s32[2]{0:T(128)S(1)} %copy-done.2, f32[64,1024]{1,0:T(8,128)S(1)} %copy-done.1, f32[64,16,128]{2,1,0:T(8,128)S(1)} %slice.32.own_ref, f32[64,16,128]{2,1,0:T(8,128)S(1)} %collective-permute-done.3.got_ref, f32[64,8,128]{2,1,0:T(8,128)S(1)} %slice.27.inv_own_ref, ...), custom_call_target="tpu_custom_call" | custom-call | tf_op jit(solution)/shard_map/final/pallas_call | solution.py:274
  109.5 2.9 %all-to-all-done.2.refs_1_ = f32[8,80,128]{2,1,0:T(8,128)S(1)} async-done(((f32[8,80,128]{2,1,0:T(8,128)}), f32[8,80,128]{2,1,0:T(8,128)S(1)}, u32[]{:S(2)}, u32[]{:S(2)}) %all-to-all-start.2) | async-done | bytes 327712 | tf_op jit(solution)/shard_map/all_to_all | solution.py:299
  112.4 0.7 copy-done.3
  113.1 3.6 %blend.1 = (f32[64,1024]{1,0:T(8,128)}, f32[16,256]{1,0:T(8,128)}) custom-call(s32[2]{0:T(128)} %pad_add_fusion.core_ref.refs_0_, f32[8,80,128]{2,1,0:T(8,128)} %copy-done.3, f32[64,1024]{1,0:T(8,128)} %refs_2_.1, f32[16,256]{1,0:T(8,128)} %refs_3_.1), custom_call_target="tpu_custom_call" | custom-call | tf_op jit(solution)/shard_map/blend/pallas_call | solution.py:245
  (19 shorter events, 0.5 us)
Async XLA Ops:
  13.8 3.6 %collective-permute-start = (f32[64,24,128]{2,1,0:T(8,128)}, f32[64,24,128]{2,1,0:T(8,128)S(1)}, u32[]{:S(2)}, u32[]{:S(2)}) collective-permute-start(f32[64,24,128]{2,1,0:T(8,128)} %get-tuple-element.17), channel_id=1, source_target_pairs={{0,8},{1,9},{2,10},{3,11},{4,12},{5,13},{6,14},{7,15},{8,0},{9,1},... | collective-permute-start | bytes 2359304 | tf_op jit(solution)/shard_map/ppermute | solution.py:295
  17.4 1.1 copy-start
  18.5 13.0 %copy-start.2 = (s32[2]{0:T(128)S(1)}, s32[2]{0:T(128)}, u32[]{:S(2)}) copy-start(s32[2]{0:T(128)} %pad_add_fusion.core_ref.refs_0_) | copy-start | bytes 28
  20.1 31.2 %all-to-all-start = ((f32[64,32,128]{2,1,0:T(8,128)}), f32[64,32,128]{2,1,0:T(8,128)S(1)}, u32[]{:S(2)}, u32[]{:S(2)}) async-start(f32[64,32,128]{2,1,0:T(8,128)} %grad_sum.1), calls=%async_computation | async-start | bytes 2097152 | tf_op jit(solution)/shard_map/all_to_all | solution.py:299
  51.3 3.6 %collective-permute-start.1 = (f32[64,40,128]{2,1,0:T(8,128)}, f32[64,40,128]{2,1,0:T(8,128)S(1)}, u32[]{:S(2)}, u32[]{:S(2)}) collective-permute-start(f32[64,40,128]{2,1,0:T(8,128)} %get-tuple-element.23), channel_id=1, source_target_pairs={{0,8},{1,9},{2,10},{3,11},{4,12},{5,13},{6,14},{7,15},{8,0},{9,1},... | collective-permute-start | bytes 3932168 | tf_op jit(solution)/shard_map/ppermute | solution.py:295
  91.0 16.2 %copy-start.1 = (f32[64,1024]{1,0:T(8,128)S(1)}, f32[64,1024]{1,0:T(8,128)}, u32[]{:S(2)}) copy-start(f32[64,1024]{1,0:T(8,128)} %inv_a_ref.1) | copy-start | bytes 786436
  91.1 16.1 %collective-permute-start.3 = (f32[64,16,128]{2,1,0:T(8,128)S(1)}, f32[64,16,128]{2,1,0:T(8,128)S(1)}, u32[]{:S(2)}, u32[]{:S(2)}) collective-permute-start(f32[64,16,128]{2,1,0:T(8,128)S(1)} %slice.32.own_ref), channel_id=1, source_target_pairs={{0,8},{1,9},{2,10},{3,11},{4,12},{5,13},{6,14},{7,15},{8,0},{9,1},... | collective-permute-start | bytes 1572872 | tf_op jit(solution)/shard_map/ppermute | solution.py:295
  93.3 1.3 %copy-start.4 = (f32[40,128]{1,0:T(8,128)}, f32[40,128]{1,0:T(8,128)S(1)}, u32[]{:S(2)}) copy-start(f32[40,128]{1,0:T(8,128)S(1)} %slice_reduce_fusion.near_ref) | copy-start | bytes 61444
  93.3 1.3 %collective-permute-start.2 = (f32[32,128]{1,0:T(8,128)S(1)}, f32[32,128]{1,0:T(8,128)S(1)}, u32[]{:S(2)}, u32[]{:S(2)}) collective-permute-start(f32[32,128]{1,0:T(8,128)S(1)} %slice.30), channel_id=1, source_target_pairs={{0,0},{1,9},{2,18},{3,27},{4,36},{5,45},{6,54},{7,63},{8,8},{9,17}... | collective-permute-start | bytes 49160 | tf_op jit(solution)/shard_map/ppermute | solution.py:295
  94.5 0.6 copy-start.5
  96.6 15.8 %all-to-all-start.2 = ((f32[8,80,128]{2,1,0:T(8,128)}), f32[8,80,128]{2,1,0:T(8,128)S(1)}, u32[]{:S(2)}, u32[]{:S(2)}) async-start(f32[8,80,128]{2,1,0:T(8,128)} %spread.1), calls=%async_computation.2 | async-start | bytes 655360 | tf_op jit(solution)/shard_map/all_to_all | solution.py:299
  104.9 2.3 %collective-permute-start.4 = (f32[64,8,128]{2,1,0:T(8,128)S(1)}, f32[64,8,128]{2,1,0:T(8,128)S(1)}, u32[]{:S(2)}, u32[]{:S(2)}) collective-permute-start(f32[64,8,128]{2,1,0:T(8,128)S(1)} %slice.27.inv_own_ref), channel_id=1, source_target_pairs={{0,8},{1,9},{2,10},{3,11},{4,12},{5,13},{6,14},{7,15},{8,0},{9,1},... | collective-permute-start | bytes 786440 | tf_op jit(solution)/shard_map/ppermute | solution.py:295
  112.4 0.7 copy-start.3

commit v5 on v4

--- a/solution.py
+++ b/solution.py
@@ -62,15 +62,18 @@
         if k + DEPTH < CHUNKS:
             for copy in copies[k + DEPTH]:
                 copy.start()
-        r = slice(k * tile, k * tile + tile)
-        gh, gl = split(gbuf[r, :])
-        ah, al = split(abuf[r, :])
-        for j in range(0, cin, 256):
-            c = slice(j, j + 256)
-            part = gram3(ah[:, c], al[:, c], gh, gl)
-            grad[c, :] = part if k == 0 else grad[c, :] + part
-        part = gram3(gh, gl, gh, gl)
-        small[...] = part if k == 0 else small[...] + part
+
+        @pl.when(core_ref[0] >= 0)
+        def _(k=k):
+            r = slice(k * tile, k * tile + tile)
+            gh, gl = split(gbuf[r, :])
+            ah, al = split(abuf[r, :])
+            for j in range(0, cin, 256):
+                c = slice(j, j + 256)
+                part = gram3(ah[:, c], al[:, c], gh, gl)
+                grad[c, :] = part if k == 0 else grad[c, :] + part
+            part = gram3(gh, gl, gh, gl)
+            small[...] = part if k == 0 else small[...] + part
 
     core = core_ref[0]
     for which, out in ((core, mine_ref), (1 - core, other_ref)):
@@ -117,19 +120,22 @@
         pltpu.make_async_copy(a_hbm.at[:, j * 256 : j * 256 + 256], buf.at[j], sems.at[j]) for j in range(count)
     ]
 
-    for copy in copies[:DEPTH]:
+    for copy in copies[:1]:
         copy.start()
     for j in range(count):
         copies[j].wait()
-        if j + DEPTH < count:
-            copies[j + DEPTH].start()
-        cj = slice(j * 256, j * 256 + 256)
-        ah[:, cj], al[:, cj] = split(buf[j])
-        for i in range(j + 1):
-            ci = slice(i * 256, i * 256 + 256)
-            acc[ci, cj] = gram3(ah[:, ci], al[:, ci], ah[:, cj], al[:, cj])
-            if i < j:
-                acc[cj, ci] = acc[ci, cj].T
+        if j + 1 < count:
+            copies[j + 1].start()
+
+        @pl.when(core_ref[0] >= 0)
+        def _(j=j):
+            cj = slice(j * 256, j * 256 + 256)
+            ah[:, cj], al[:, cj] = split(buf[j])
+            for i in range(j + 1):
+                ci = slice(i * 256, i * 256 + 256)
+                acc[ci, cj] = gram3(ah[:, ci], al[:, ci], ah[:, cj], al[:, cj])
+                if i < j:
+                    acc[cj, ci] = acc[ci, cj].T
 
     low = lax.broadcasted_iota(jnp.int32, (32, 128), 1) < 64
     for side in range(2):
@@ -176,18 +182,18 @@
 def pack_kernel(mine_ref, got_ref, tail_ref, out_ref):
     lead = mine_ref.shape[1]
     out_ref[:, :lead, :] = mine_ref[...] + got_ref[...]
+    extra = out_ref.shape[1] - lead
     for i in range(out_ref.shape[0]):
-        out_ref[i, lead:, :] = tail_ref[...]
-
-
-def pack(mine, got, tail, name):
+        out_ref[i, lead:, :] = tail_ref[:extra, :]
+
+
+def pack(mine, got, tail, extra, name):
     chunks, lead, lanes = mine.shape
-    extra = tail.shape[0]
     spec = pl.BlockSpec((chunks // 4, lead, lanes), lambda i: (i, 0, 0))
     return pl.pallas_call(
         pack_kernel,
         grid=(4,),
-        in_specs=[spec, spec, pl.BlockSpec((extra, lanes), lambda i: (0, 0))],
+        in_specs=[spec, spec, pl.BlockSpec(tail.shape, lambda i: (0, 0))],
         out_specs=pl.BlockSpec((chunks // 4, lead + extra, lanes), lambda i: (i, 0, 0)),
         out_shape=jax.ShapeDtypeStruct((chunks, lead + extra, lanes), F32),
         compiler_params=pltpu.CompilerParams(vmem_limit_bytes=16 * 2**20),
@@ -200,20 +206,21 @@
         out_ref[r, :32, :] = near_ref[:32, :]
         out_ref[r, 32:64, :] = mirror_ref[...]
         out_ref[r, 64:72, :] = near_ref[32:40, :]
-        out_ref[r, 72:, :] = tile_ref[...]
+        out_ref[r, 72:, :] = tile_ref[16:, :]
 
 
 def spread(near, mirror, tile):
     return pl.pallas_call(
         spread_kernel,
         out_shape=jax.ShapeDtypeStruct((8, 80, 128), F32),
+        compiler_params=pltpu.CompilerParams(vmem_limit_bytes=16 * 2**20),
         name="spread",
     )(near, mirror, tile)
 
 
 def blend_kernel(place_ref, rows_ref, fa_ref, fg_ref, na_ref, ng_ref, stat, *, total_rows):
     keep, fresh = decay_rate, 1.0 - decay_rate
-    panel = place_ref[1]
+    panel = place_ref[0]
     for c in range(16):
         cols = slice(64 * c, 64 * c + 64)
         k = (c - panel + 16) % 16
@@ -248,6 +255,7 @@
         out_specs=[in_vmem()] * 2,
         out_shape=[jax.ShapeDtypeStruct(factor_a.shape, F32), jax.ShapeDtypeStruct(factor_g.shape, F32)],
         scratch_shapes=[pltpu.VMEM(factor_a.shape, F32)],
+        compiler_params=pltpu.CompilerParams(vmem_limit_bytes=16 * 2**20),
         name="blend",
     )(place, rows, factor_a, factor_g)
 
@@ -301,12 +309,13 @@
 
 def local(activations, out_grads, factor_a, factor_g, inverse_a, inverse_g):
     total_rows = activations.shape[0] * 128
-    core = jnp.stack([lax.axis_index("co"), lax.axis_index(("x", "zl", "co"))]).astype(jnp.int32)
+    core = lax.axis_index("co").astype(jnp.int32).reshape(1)
+    place = lax.axis_index(("x", "zl", "co")).astype(jnp.int32).reshape(1)
     y = lax.axis_index("y")
 
     g_mine, g_other = grad_parts(core, activations, out_grads)
     tile = lax.dynamic_slice(inverse_g, (8 * (y // 2), 128 * (y % 2)), (8, 128))
-    g_sum = pack(g_mine, swap(g_other), tile, "grad_sum")
+    g_sum = pack(g_mine, swap(g_other), tile, 8, "grad_sum")
     g_sum, core = lax.optimization_barrier((g_sum, core))
     g_all = exchange(g_sum, CHIPS)
 
@@ -314,18 +323,19 @@
     g_all, s_mine, s_other = lax.optimization_barrier((g_all, s_mine, s_other))
     g_own = jnp.sum(g_all[:, :24], axis=0)
     inv_own = g_all[:, 24:]
-    s_sum = pack(s_mine, swap(s_other), g_own[:16], "stat_sum")
+    inv_got = swap(inv_own)
+    s_sum = pack(s_mine, swap(s_other), g_own, 16, "stat_sum")
+    s_sum, inv_got = lax.optimization_barrier((s_sum, inv_got))
     s_all = exchange(s_sum, CHIPS)
-    inv_got = swap(inv_own)
 
     near = jnp.sum(s_all[:, :40], axis=0)
     mirror = swap(near[:32], across)
     own = s_all[:, 40:]
     got = swap(own)
-    rows = exchange(spread(near, mirror, g_own[16:]), ("y", "zh"))
+    rows = exchange(spread(near, mirror, g_own), ("y", "zh"))
     precond_grad = final(core, inverse_a, own, got, inv_own, inv_got)
     rows, precond_grad = lax.optimization_barrier((rows, precond_grad))
-    new_factor_a, new_factor_g = blend(core, rows, factor_a, factor_g, total_rows)
+    new_factor_a, new_factor_g = blend(place, rows, factor_a, factor_g, total_rows)
     return new_factor_a, new_factor_g, precond_grad
 
 

time: 118 us -> 112 us (0.949)
  Pallas kernels: 41.5 us -> 35.9 us
  waiting for transfers between devices: 8.27 us -> 10.2 us
  local copies, waits for them, and re-layouts: 3.83 us -> 1.91 us
    all_to_all x2, waiting for transfers between devices: 2.88 us -> 5.75 us  [exchange(): return lax.all_to_all(array, axes, 0, 0, tiled=True)]
    pallas_call x1, Pallas kernels: 12.5 us -> 10.6 us  [grad_parts(): pl.pallas_call(grad_kernel, in_specs=[in_smem(), in_hbm(), in_hbm()], out...]
    unnamed x12 -> x8, local copies, waits for them, and re-layouts: 2.47 us -> 1.15 us
    pallas_call x1, Pallas kernels: 19.8 us -> 18.5 us  [stat_parts(): pl.pallas_call(stat_kernel, in_specs=[in_smem(), in_hbm()], out_specs=[in...]
  transfers between devices with their start and end apart: 7 -> 7, of which waited for: 4 -> 3; matrix products, arithmetic and copies ran while one was open for 1% -> 1% of each run, Pallas kernels for 20% -> 19%
where the time goes in v5:
time: 112 us; the launch traced here: 110 us
  Pallas kernels  35.9 us (32%)
  blocking collectives  35.3 us (32%)
  starting transfers between devices  25.6 us (23%)
  waiting for transfers between devices  10.2 us (9%)
  local copies, waits for them, and re-layouts  1.91 us (2%)
    all_to_all x1, blocking collectives, exchange(): return lax.all_to_all(array, axes, 0, 0, tiled=True)  35.3 us
    all_to_all x2, starting transfers between devices, exchange(): return lax.all_to_all(array, axes, 0, 0, tiled=True)  20 us
    pallas_call x1, Pallas kernels, stat_parts(): pl.pallas_call(stat_kernel, in_specs=[in_smem(), in_hbm()], out_specs=[in...  18.5 us
    pallas_call x1, Pallas kernels, grad_parts(): pl.pallas_call(grad_kernel, in_specs=[in_smem(), in_hbm(), in_hbm()], out...  10.6 us
    all_to_all x2, waiting for transfers between devices, exchange(): return lax.all_to_all(array, axes, 0, 0, tiled=True)  5.75 us
    ppermute x5, starting transfers between devices, swap(): return lax.ppermute(array, SUB, [(i, to(i)) for i in range(128)])  5.59 us
    ppermute x5, waiting for transfers between devices, swap(): return lax.ppermute(array, SUB, [(i, to(i)) for i in range(128)])  4.48 us
    pallas_call x1, Pallas kernels, blend(): pl.pallas_call(lambda *refs: blend_kernel(*refs, total_rows=total_rows),...  2.52 us
  transfers between devices with their start and end apart: 7, of which 3 were waited for; matrix products, arithmetic and copies ran while one was open for 1% of the time, Pallas kernels for 19%

profile of v5, /device:TPU:1, one launch (start us, length us, event | category | flops | bytes accessed | tf_op | source)
XLA Modules:
  0.0 110.0 jit_solution(17358257094322962284)
XLA Ops:
  0.6 10.6 %grad_parts.1 = (f32[64,24,128]{2,1,0:T(8,128)}, f32[64,24,128]{2,1,0:T(8,128)}) custom-call(s32[1]{0:T(128)} %bitcast.1.core_ref, f32[3072,1024]{1,0:T(8,128)} %a_hbm.3, f32[3072,256]{1,0:T(8,128)} %g_hbm.1), custom_call_target="tpu_custom_call" | custom-call | flops 6039797760 | bytes 15728640 | tf_op jit(solution)/shard_map/grad_parts/pallas_call | solution.py:98
  11.3 1.5 %collective-permute-start = (f32[64,24,128]{2,1,0:T(8,128)}, f32[64,24,128]{2,1,0:T(8,128)S(1)}, u32[]{:S(2)}, u32[]{:S(2)}) collective-permute-start(f32[64,24,128]{2,1,0:T(8,128)} %get-tuple-element.19), channel_id=1, source_target_pairs={{0,8},{1,9},{2,10},{3,11},{4,12},{5,13},{6,14},{7,15},{8,0},{9,1},... | collective-permute-start | bytes 2359304 | tf_op jit(solution)/shard_map/ppermute | solution.py:303
  12.8 0.7 dynamic_slice.3.tail_ref
  13.5 1.4 %collective-permute-done.got_ref = f32[64,24,128]{2,1,0:T(8,128)S(1)} collective-permute-done((f32[64,24,128]{2,1,0:T(8,128)}, f32[64,24,128]{2,1,0:T(8,128)S(1)}, u32[]{:S(2)}, u32[]{:S(2)}) %collective-permute-start) | collective-permute-done | bytes 786464 | tf_op jit(solution)/shard_map/ppermute | solution.py:303
  14.9 1.1 %copy-done = f32[64,24,128]{2,1,0:T(8,128)S(1)} copy-done((f32[64,24,128]{2,1,0:T(8,128)S(1)}, f32[64,24,128]{2,1,0:T(8,128)}, u32[]{:S(2)}) %copy-start) | copy-done | bytes 786456
  16.0 1.6 %grad_sum.1 = f32[64,32,128]{2,1,0:T(8,128)} custom-call(f32[64,24,128]{2,1,0:T(8,128)S(1)} %copy-done, f32[64,24,128]{2,1,0:T(8,128)S(1)} %collective-permute-done.got_ref, f32[8,128]{1,0:T(8,128)S(1)} %dynamic_slice.3.tail_ref), custom_call_target="tpu_custom_call" | custom-call | tf_op jit(solution)/shard_map/grad_sum/pallas_call | solution.py:193
  17.6 11.2 %all-to-all-start = ((f32[64,32,128]{2,1,0:T(8,128)}), f32[64,32,128]{2,1,0:T(8,128)S(1)}, u32[]{:S(2)}, u32[]{:S(2)}) async-start(f32[64,32,128]{2,1,0:T(8,128)} %grad_sum.1), calls=%async_computation | async-start | bytes 2097152 | tf_op jit(solution)/shard_map/all_to_all | solution.py:307
  28.8 18.5 %stat_parts.1 = (f32[64,40,128]{2,1,0:T(8,128)S(1)}, f32[64,40,128]{2,1,0:T(8,128)}) custom-call(s32[1]{0:T(128)} %bitcast.1.core_ref, f32[3072,1024]{1,0:T(8,128)} %a_hbm.3), custom_call_target="tpu_custom_call" | custom-call | flops 12884901888 | bytes 12582912 | tf_op jit(solution)/shard_map/stat_parts/pallas_call | solution.py:164
  47.3 1.2 %collective-permute-start.1 = (f32[64,40,128]{2,1,0:T(8,128)}, f32[64,40,128]{2,1,0:T(8,128)S(1)}, u32[]{:S(2)}, u32[]{:S(2)}) collective-permute-start(f32[64,40,128]{2,1,0:T(8,128)} %get-tuple-element.25), channel_id=1, source_target_pairs={{0,8},{1,9},{2,10},{3,11},{4,12},{5,13},{6,14},{7,15},{8,0},{9,1},... | collective-permute-start | bytes 3932168 | tf_op jit(solution)/shard_map/ppermute | solution.py:303
  48.6 0.1 collective-permute-start.2
  48.7 0.1 slice_reduce_fusion.1.tail_ref.tile_ref
  48.8 3.0 %collective-permute-done.1.got_ref = f32[64,40,128]{2,1,0:T(8,128)S(1)} collective-permute-done((f32[64,40,128]{2,1,0:T(8,128)}, f32[64,40,128]{2,1,0:T(8,128)S(1)}, u32[]{:S(2)}, u32[]{:S(2)}) %collective-permute-start.1) | collective-permute-done | bytes 1310752 | tf_op jit(solution)/shard_map/ppermute | solution.py:303
  51.8 0.2 stat_sum.1
  52.1 35.3 %all_to_all.15 = f32[64,56,128]{2,1,0:T(8,128)S(1)} all-to-all(f32[64,56,128]{2,1,0:T(8,128)S(1)} %stat_sum.1), channel_id=1, replica_groups=mesh['x'=4,'zl'=2,'co'=2,'y'=4,'zh'=2] {'x','zl','y','zh'}, dimensions={0} | all-to-all | bytes 3670016 | tf_op jit(solution)/shard_map/all_to_all | solution.py:307
  87.4 0.0 copy-start.1
  87.4 0.0 copy-start.3
  87.5 2.1 %collective-permute-start.4 = (f32[64,16,128]{2,1,0:T(8,128)S(1)}, f32[64,16,128]{2,1,0:T(8,128)S(1)}, u32[]{:S(2)}, u32[]{:S(2)}) collective-permute-start(f32[64,16,128]{2,1,0:T(8,128)S(1)} %slice.22.own_ref), channel_id=1, source_target_pairs={{0,8},{1,9},{2,10},{3,11},{4,12},{5,13},{6,14},{7,15},{8,0},{9,1},... | collective-permute-start | bytes 1572872 | tf_op jit(solution)/shard_map/ppermute | solution.py:303
  89.6 0.1 slice_reduce_fusion.near_ref
  89.7 0.7 collective-permute-start.3
  90.3 0.8 spread.1
  91.1 8.8 %all-to-all-start.2 = ((f32[8,80,128]{2,1,0:T(8,128)}), f32[8,80,128]{2,1,0:T(8,128)S(1)}, u32[]{:S(2)}, u32[]{:S(2)}) async-start(f32[8,80,128]{2,1,0:T(8,128)} %spread.1), calls=%async_computation.2 | async-start | bytes 655360 | tf_op jit(solution)/shard_map/all_to_all | solution.py:307
  99.9 1.8 %final.1 = f32[64,256]{1,0:T(8,128)} custom-call(s32[1]{0:T(128)} %bitcast.1.core_ref, f32[64,1024]{1,0:T(8,128)S(1)} %copy-done.2, f32[64,16,128]{2,1,0:T(8,128)S(1)} %slice.22.own_ref, f32[64,16,128]{2,1,0:T(8,128)S(1)} %collective-permute-done.4.got_ref, f32[64,8,128]{2,1,0:T(8,128)S(1)} %slice.16.inv_own_ref, ...), custom_call_target="tpu_custom_call" | custom-call | tf_op jit(solution)/shard_map/final/pallas_call | solution.py:282
  101.7 5.7 %all-to-all-done.2.refs_1_ = f32[8,80,128]{2,1,0:T(8,128)S(1)} async-done(((f32[8,80,128]{2,1,0:T(8,128)}), f32[8,80,128]{2,1,0:T(8,128)S(1)}, u32[]{:S(2)}, u32[]{:S(2)}) %all-to-all-start.2) | async-done | bytes 327712 | tf_op jit(solution)/shard_map/all_to_all | solution.py:307
  107.5 2.5 %blend.1 = (f32[64,1024]{1,0:T(8,128)}, f32[16,256]{1,0:T(8,128)}) custom-call(s32[1]{0:T(128)} %bitcast.refs_0_, f32[8,80,128]{2,1,0:T(8,128)S(1)} %all-to-all-done.2.refs_1_, f32[64,1024]{1,0:T(8,128)S(1)} %copy-done.1, f32[16,256]{1,0:T(8,128)S(1)} %copy-done.3), custom_call_target="tpu_custom_call" | custom-call | tf_op jit(solution)/shard_map/blend/pallas_call | solution.py:252
  (12 shorter events, 0.1 us)
Async XLA Ops:
  11.3 3.6 %collective-permute-start = (f32[64,24,128]{2,1,0:T(8,128)}, f32[64,24,128]{2,1,0:T(8,128)S(1)}, u32[]{:S(2)}, u32[]{:S(2)}) collective-permute-start(f32[64,24,128]{2,1,0:T(8,128)} %get-tuple-element.19), channel_id=1, source_target_pairs={{0,8},{1,9},{2,10},{3,11},{4,12},{5,13},{6,14},{7,15},{8,0},{9,1},... | collective-permute-start | bytes 2359304 | tf_op jit(solution)/shard_map/ppermute | solution.py:303
  14.9 1.1 %copy-start = (f32[64,24,128]{2,1,0:T(8,128)S(1)}, f32[64,24,128]{2,1,0:T(8,128)}, u32[]{:S(2)}) copy-start(f32[64,24,128]{2,1,0:T(8,128)} %get-tuple-element.18.mine_ref) | copy-start | bytes 2359300
  17.6 29.7 %all-to-all-start = ((f32[64,32,128]{2,1,0:T(8,128)}), f32[64,32,128]{2,1,0:T(8,128)S(1)}, u32[]{:S(2)}, u32[]{:S(2)}) async-start(f32[64,32,128]{2,1,0:T(8,128)} %grad_sum.1), calls=%async_computation | async-start | bytes 2097152 | tf_op jit(solution)/shard_map/all_to_all | solution.py:307
  47.3 4.5 %collective-permute-start.1 = (f32[64,40,128]{2,1,0:T(8,128)}, f32[64,40,128]{2,1,0:T(8,128)S(1)}, u32[]{:S(2)}, u32[]{:S(2)}) collective-permute-start(f32[64,40,128]{2,1,0:T(8,128)} %get-tuple-element.25), channel_id=1, source_target_pairs={{0,8},{1,9},{2,10},{3,11},{4,12},{5,13},{6,14},{7,15},{8,0},{9,1},... | collective-permute-start | bytes 3932168 | tf_op jit(solution)/shard_map/ppermute | solution.py:303
  48.6 3.4 %collective-permute-start.2 = (f32[64,8,128]{2,1,0:T(8,128)S(1)}, f32[64,8,128]{2,1,0:T(8,128)S(1)}, u32[]{:S(2)}, u32[]{:S(2)}) collective-permute-start(f32[64,8,128]{2,1,0:T(8,128)S(1)} %slice.16.inv_own_ref), channel_id=1, source_target_pairs={{0,8},{1,9},{2,10},{3,11},{4,12},{5,13},{6,14},{7,15},{8,0},{9,1},... | collective-permute-start | bytes 786440 | tf_op jit(solution)/shard_map/ppermute | solution.py:303
  87.4 12.5 %copy-start.2 = (f32[64,1024]{1,0:T(8,128)S(1)}, f32[64,1024]{1,0:T(8,128)}, u32[]{:S(2)}) copy-start(f32[64,1024]{1,0:T(8,128)} %inv_a_ref.1) | copy-start | bytes 786436
  87.4 20.0 %copy-start.1 = (f32[64,1024]{1,0:T(8,128)S(1)}, f32[64,1024]{1,0:T(8,128)}, u32[]{:S(2)}) copy-start(f32[64,1024]{1,0:T(8,128)} %refs_2_.1) | copy-start | bytes 786436
  87.4 20.0 %copy-start.3 = (f32[16,256]{1,0:T(8,128)S(1)}, f32[16,256]{1,0:T(8,128)}, u32[]{:S(2)}) copy-start(f32[16,256]{1,0:T(8,128)} %refs_3_.1) | copy-start | bytes 49156
  87.5 12.4 %collective-permute-start.4 = (f32[64,16,128]{2,1,0:T(8,128)S(1)}, f32[64,16,128]{2,1,0:T(8,128)S(1)}, u32[]{:S(2)}, u32[]{:S(2)}) collective-permute-start(f32[64,16,128]{2,1,0:T(8,128)S(1)} %slice.22.own_ref), channel_id=1, source_target_pairs={{0,8},{1,9},{2,10},{3,11},{4,12},{5,13},{6,14},{7,15},{8,0},{9,1},... | collective-permute-start | bytes 1572872 | tf_op jit(solution)/shard_map/ppermute | solution.py:303
  89.7 0.7 collective-permute-start.3
  91.1 16.4 %all-to-all-start.2 = ((f32[8,80,128]{2,1,0:T(8,128)}), f32[8,80,128]{2,1,0:T(8,128)S(1)}, u32[]{:S(2)}, u32[]{:S(2)}) async-start(f32[8,80,128]{2,1,0:T(8,128)} %spread.1), calls=%async_computation.2 | async-start | bytes 655360 | tf_op jit(solution)/shard_map/all_to_all | solution.py:307

commit v6 on v5

--- a/solution.py
+++ b/solution.py
@@ -113,7 +113,7 @@
     )(core, activations, out_grads)
 
 
-def stat_kernel(core_ref, a_hbm, mine_ref, other_ref, buf, ah, al, acc, sems):
+def stat_kernel(core_ref, a_hbm, mine_ref, other_ref, buf, ah, al, acc, cross, sems):
     cin = acc.shape[0]
     count = cin // 256
     copies = [
@@ -131,11 +131,18 @@
         def _(j=j):
             cj = slice(j * 256, j * 256 + 256)
             ah[:, cj], al[:, cj] = split(buf[j])
-            for i in range(j + 1):
+            cross[j] = gram(ah[:, cj], al[:, cj])
+            acc[cj, cj] = gram(ah[:, cj], ah[:, cj])
+            for i in range(j):
                 ci = slice(i * 256, i * 256 + 256)
                 acc[ci, cj] = gram3(ah[:, ci], al[:, ci], ah[:, cj], al[:, cj])
-                if i < j:
-                    acc[cj, ci] = acc[ci, cj].T
+                acc[cj, ci] = acc[ci, cj].T
+
+    @pl.when(core_ref[0] >= 0)
+    def _():
+        for j in range(count):
+            cj = slice(j * 256, j * 256 + 256)
+            acc[cj, cj] = acc[cj, cj] + (cross[j] + cross[j].T)
 
     low = lax.broadcasted_iota(jnp.int32, (32, 128), 1) < 64
     for side in range(2):
@@ -171,6 +178,7 @@
             pltpu.VMEM((rows, cin), BF16),
             pltpu.VMEM((rows, cin), BF16),
             pltpu.VMEM((cin, cin), F32),
+            pltpu.VMEM((cin // 256, 256, 256), F32),
             pltpu.SemaphoreType.DMA((cin // 256,)),
         ],
         compiler_params=pltpu.CompilerParams(vmem_limit_bytes=52 * 2**20),

time: 112 us -> 111 us (level)
  blocking collectives: 35.3 us -> 34.1 us
    pallas_call x1, Pallas kernels: 18.5 us -> 17.3 us  [stat_parts(): pl.pallas_call(stat_kernel, in_specs=[in_smem(), in_hbm()], out_specs=[in...]
    all_to_all x1, blocking collectives: 35.3 us -> 34.1 us  [exchange(): return lax.all_to_all(array, axes, 0, 0, tiled=True)]
  transfers between devices with their start and end apart: 7 -> 7, of which waited for: 3 -> 4; matrix products, arithmetic and copies ran while one was open for 1% -> 1% of each run, Pallas kernels for 19% -> 18%
where the time goes in v6:
time: 111 us; the launch traced here: 109 us
  Pallas kernels  34.8 us (31%)
  blocking collectives  34.1 us (31%)
  starting transfers between devices  26.4 us (24%)
  waiting for transfers between devices  10.7 us (10%)
  local copies, waits for them, and re-layouts  1.91 us (2%)
    all_to_all x1, blocking collectives, exchange(): return lax.all_to_all(array, axes, 0, 0, tiled=True)  34.1 us
    all_to_all x2, starting transfers between devices, exchange(): return lax.all_to_all(array, axes, 0, 0, tiled=True)  20 us
    pallas_call x1, Pallas kernels, stat_parts(): pl.pallas_call(stat_kernel, in_specs=[in_smem(), in_hbm()], out_specs=[in...  17.3 us
    pallas_call x1, Pallas kernels, grad_parts(): pl.pallas_call(grad_kernel, in_specs=[in_smem(), in_hbm(), in_hbm()], out...  10.6 us
    ppermute x5, starting transfers between devices, swap(): return lax.ppermute(array, SUB, [(i, to(i)) for i in range(128)])  6.34 us
    all_to_all x2, waiting for transfers between devices, exchange(): return lax.all_to_all(array, axes, 0, 0, tiled=True)  6.2 us
    ppermute x5, waiting for transfers between devices, swap(): return lax.ppermute(array, SUB, [(i, to(i)) for i in range(128)])  4.48 us
    pallas_call x1, Pallas kernels, blend(): pl.pallas_call(lambda *refs: blend_kernel(*refs, total_rows=total_rows),...  2.52 us
  transfers between devices with their start and end apart: 7, of which 4 were waited for; matrix products, arithmetic and copies ran while one was open for 1% of the time, Pallas kernels for 18%

profile of v6, /device:TPU:1, one launch (start us, length us, event | category | flops | bytes accessed | tf_op | source)
XLA Modules:
  0.0 108.8 jit_solution(14830051261522760695)
XLA Ops:
  0.6 10.6 %grad_parts.1 = (f32[64,24,128]{2,1,0:T(8,128)}, f32[64,24,128]{2,1,0:T(8,128)}) custom-call(s32[1]{0:T(128)} %bitcast.1.core_ref, f32[3072,1024]{1,0:T(8,128)} %a_hbm.3, f32[3072,256]{1,0:T(8,128)} %g_hbm.1), custom_call_target="tpu_custom_call" | custom-call | flops 6039797760 | bytes 15728640 | tf_op jit(solution)/shard_map/grad_parts/pallas_call | solution.py:98
  11.3 1.5 %collective-permute-start = (f32[64,24,128]{2,1,0:T(8,128)}, f32[64,24,128]{2,1,0:T(8,128)S(1)}, u32[]{:S(2)}, u32[]{:S(2)}) collective-permute-start(f32[64,24,128]{2,1,0:T(8,128)} %get-tuple-element.19), channel_id=1, source_target_pairs={{0,8},{1,9},{2,10},{3,11},{4,12},{5,13},{6,14},{7,15},{8,0},{9,1},... | collective-permute-start | bytes 2359304 | tf_op jit(solution)/shard_map/ppermute | solution.py:311
  12.8 0.7 dynamic_slice.3.tail_ref
  13.5 1.4 %collective-permute-done.got_ref = f32[64,24,128]{2,1,0:T(8,128)S(1)} collective-permute-done((f32[64,24,128]{2,1,0:T(8,128)}, f32[64,24,128]{2,1,0:T(8,128)S(1)}, u32[]{:S(2)}, u32[]{:S(2)}) %collective-permute-start) | collective-permute-done | bytes 786464 | tf_op jit(solution)/shard_map/ppermute | solution.py:311
  14.9 1.1 %copy-done = f32[64,24,128]{2,1,0:T(8,128)S(1)} copy-done((f32[64,24,128]{2,1,0:T(8,128)S(1)}, f32[64,24,128]{2,1,0:T(8,128)}, u32[]{:S(2)}) %copy-start) | copy-done | bytes 786456
  16.0 1.6 %grad_sum.1 = f32[64,32,128]{2,1,0:T(8,128)} custom-call(f32[64,24,128]{2,1,0:T(8,128)S(1)} %copy-done, f32[64,24,128]{2,1,0:T(8,128)S(1)} %collective-permute-done.got_ref, f32[8,128]{1,0:T(8,128)S(1)} %dynamic_slice.3.tail_ref), custom_call_target="tpu_custom_call" | custom-call | tf_op jit(solution)/shard_map/grad_sum/pallas_call | solution.py:201
  17.6 11.2 %all-to-all-start = ((f32[64,32,128]{2,1,0:T(8,128)}), f32[64,32,128]{2,1,0:T(8,128)S(1)}, u32[]{:S(2)}, u32[]{:S(2)}) async-start(f32[64,32,128]{2,1,0:T(8,128)} %grad_sum.1), calls=%async_computation | async-start | bytes 2097152 | tf_op jit(solution)/shard_map/all_to_all | solution.py:315
  28.8 17.3 %stat_parts.1 = (f32[64,40,128]{2,1,0:T(8,128)S(1)}, f32[64,40,128]{2,1,0:T(8,128)}) custom-call(s32[1]{0:T(128)} %bitcast.1.core_ref, f32[3072,1024]{1,0:T(8,128)} %a_hbm.3), custom_call_target="tpu_custom_call" | custom-call | flops 12884901888 | bytes 12582912 | tf_op jit(solution)/shard_map/stat_parts/pallas_call | solution.py:171
  46.1 0.5 all-to-all-done
  46.6 2.0 %collective-permute-start.1 = (f32[64,40,128]{2,1,0:T(8,128)}, f32[64,40,128]{2,1,0:T(8,128)S(1)}, u32[]{:S(2)}, u32[]{:S(2)}) collective-permute-start(f32[64,40,128]{2,1,0:T(8,128)} %get-tuple-element.25), channel_id=1, source_target_pairs={{0,8},{1,9},{2,10},{3,11},{4,12},{5,13},{6,14},{7,15},{8,0},{9,1},... | collective-permute-start | bytes 3932168 | tf_op jit(solution)/shard_map/ppermute | solution.py:311
  48.6 0.1 collective-permute-start.2
  48.7 0.1 slice_reduce_fusion.1.tail_ref.tile_ref
  48.8 3.0 %collective-permute-done.1.got_ref = f32[64,40,128]{2,1,0:T(8,128)S(1)} collective-permute-done((f32[64,40,128]{2,1,0:T(8,128)}, f32[64,40,128]{2,1,0:T(8,128)S(1)}, u32[]{:S(2)}, u32[]{:S(2)}) %collective-permute-start.1) | collective-permute-done | bytes 1310752 | tf_op jit(solution)/shard_map/ppermute | solution.py:311
  51.8 0.2 stat_sum.1
  52.1 34.1 %all_to_all.15 = f32[64,56,128]{2,1,0:T(8,128)S(1)} all-to-all(f32[64,56,128]{2,1,0:T(8,128)S(1)} %stat_sum.1), channel_id=1, replica_groups=mesh['x'=4,'zl'=2,'co'=2,'y'=4,'zh'=2] {'x','zl','y','zh'}, dimensions={0} | all-to-all | bytes 3670016 | tf_op jit(solution)/shard_map/all_to_all | solution.py:315
  86.2 0.0 copy-start.1
  86.3 2.1 %collective-permute-start.4 = (f32[64,16,128]{2,1,0:T(8,128)S(1)}, f32[64,16,128]{2,1,0:T(8,128)S(1)}, u32[]{:S(2)}, u32[]{:S(2)}) collective-permute-start(f32[64,16,128]{2,1,0:T(8,128)S(1)} %slice.22.own_ref), channel_id=1, source_target_pairs={{0,8},{1,9},{2,10},{3,11},{4,12},{5,13},{6,14},{7,15},{8,0},{9,1},... | collective-permute-start | bytes 1572872 | tf_op jit(solution)/shard_map/ppermute | solution.py:311
  88.4 0.1 slice_reduce_fusion.near_ref
  88.5 0.7 collective-permute-start.3
  89.2 0.8 spread.1
  89.9 8.8 %all-to-all-start.2 = ((f32[8,80,128]{2,1,0:T(8,128)}), f32[8,80,128]{2,1,0:T(8,128)S(1)}, u32[]{:S(2)}, u32[]{:S(2)}) async-start(f32[8,80,128]{2,1,0:T(8,128)} %spread.1), calls=%async_computation.2 | async-start | bytes 655360 | tf_op jit(solution)/shard_map/all_to_all | solution.py:315
  98.7 1.8 %final.1 = f32[64,256]{1,0:T(8,128)} custom-call(s32[1]{0:T(128)} %bitcast.1.core_ref, f32[64,1024]{1,0:T(8,128)S(1)} %copy-done.2, f32[64,16,128]{2,1,0:T(8,128)S(1)} %slice.22.own_ref, f32[64,16,128]{2,1,0:T(8,128)S(1)} %collective-permute-done.4.got_ref, f32[64,8,128]{2,1,0:T(8,128)S(1)} %slice.16.inv_own_ref, ...), custom_call_target="tpu_custom_call" | custom-call | tf_op jit(solution)/shard_map/final/pallas_call | solution.py:290
  100.5 5.7 %all-to-all-done.2.refs_1_ = f32[8,80,128]{2,1,0:T(8,128)S(1)} async-done(((f32[8,80,128]{2,1,0:T(8,128)}), f32[8,80,128]{2,1,0:T(8,128)S(1)}, u32[]{:S(2)}, u32[]{:S(2)}) %all-to-all-start.2) | async-done | bytes 327712 | tf_op jit(solution)/shard_map/all_to_all | solution.py:315
  106.3 2.5 %blend.1 = (f32[64,1024]{1,0:T(8,128)}, f32[16,256]{1,0:T(8,128)}) custom-call(s32[1]{0:T(128)} %bitcast.refs_0_, f32[8,80,128]{2,1,0:T(8,128)S(1)} %all-to-all-done.2.refs_1_, f32[64,1024]{1,0:T(8,128)S(1)} %copy-done.1, f32[16,256]{1,0:T(8,128)S(1)} %copy-done.3), custom_call_target="tpu_custom_call" | custom-call | tf_op jit(solution)/shard_map/blend/pallas_call | solution.py:260
  (12 shorter events, 0.1 us)
Async XLA Ops:
  11.3 3.6 %collective-permute-start = (f32[64,24,128]{2,1,0:T(8,128)}, f32[64,24,128]{2,1,0:T(8,128)S(1)}, u32[]{:S(2)}, u32[]{:S(2)}) collective-permute-start(f32[64,24,128]{2,1,0:T(8,128)} %get-tuple-element.19), channel_id=1, source_target_pairs={{0,8},{1,9},{2,10},{3,11},{4,12},{5,13},{6,14},{7,15},{8,0},{9,1},... | collective-permute-start | bytes 2359304 | tf_op jit(solution)/shard_map/ppermute | solution.py:311
  14.9 1.1 %copy-start = (f32[64,24,128]{2,1,0:T(8,128)S(1)}, f32[64,24,128]{2,1,0:T(8,128)}, u32[]{:S(2)}) copy-start(f32[64,24,128]{2,1,0:T(8,128)} %get-tuple-element.18.mine_ref) | copy-start | bytes 2359300
  17.6 29.0 %all-to-all-start = ((f32[64,32,128]{2,1,0:T(8,128)}), f32[64,32,128]{2,1,0:T(8,128)S(1)}, u32[]{:S(2)}, u32[]{:S(2)}) async-start(f32[64,32,128]{2,1,0:T(8,128)} %grad_sum.1), calls=%async_computation | async-start | bytes 2097152 | tf_op jit(solution)/shard_map/all_to_all | solution.py:315
  46.6 5.2 %collective-permute-start.1 = (f32[64,40,128]{2,1,0:T(8,128)}, f32[64,40,128]{2,1,0:T(8,128)S(1)}, u32[]{:S(2)}, u32[]{:S(2)}) collective-permute-start(f32[64,40,128]{2,1,0:T(8,128)} %get-tuple-element.25), channel_id=1, source_target_pairs={{0,8},{1,9},{2,10},{3,11},{4,12},{5,13},{6,14},{7,15},{8,0},{9,1},... | collective-permute-start | bytes 3932168 | tf_op jit(solution)/shard_map/ppermute | solution.py:311
  48.6 3.4 %collective-permute-start.2 = (f32[64,8,128]{2,1,0:T(8,128)S(1)}, f32[64,8,128]{2,1,0:T(8,128)S(1)}, u32[]{:S(2)}, u32[]{:S(2)}) collective-permute-start(f32[64,8,128]{2,1,0:T(8,128)S(1)} %slice.16.inv_own_ref), channel_id=1, source_target_pairs={{0,8},{1,9},{2,10},{3,11},{4,12},{5,13},{6,14},{7,15},{8,0},{9,1},... | collective-permute-start | bytes 786440 | tf_op jit(solution)/shard_map/ppermute | solution.py:311
  86.2 12.5 %copy-start.2 = (f32[64,1024]{1,0:T(8,128)S(1)}, f32[64,1024]{1,0:T(8,128)}, u32[]{:S(2)}) copy-start(f32[64,1024]{1,0:T(8,128)} %inv_a_ref.1) | copy-start | bytes 786436
  86.2 20.0 %copy-start.1 = (f32[64,1024]{1,0:T(8,128)S(1)}, f32[64,1024]{1,0:T(8,128)}, u32[]{:S(2)}) copy-start(f32[64,1024]{1,0:T(8,128)} %refs_2_.1) | copy-start | bytes 786436
  86.3 20.0 %copy-start.3 = (f32[16,256]{1,0:T(8,128)S(1)}, f32[16,256]{1,0:T(8,128)}, u32[]{:S(2)}) copy-start(f32[16,256]{1,0:T(8,128)} %refs_3_.1) | copy-start | bytes 49156
  86.3 12.4 %collective-permute-start.4 = (f32[64,16,128]{2,1,0:T(8,128)S(1)}, f32[64,16,128]{2,1,0:T(8,128)S(1)}, u32[]{:S(2)}, u32[]{:S(2)}) collective-permute-start(f32[64,16,128]{2,1,0:T(8,128)S(1)} %slice.22.own_ref), channel_id=1, source_target_pairs={{0,8},{1,9},{2,10},{3,11},{4,12},{5,13},{6,14},{7,15},{8,0},{9,1},... | collective-permute-start | bytes 1572872 | tf_op jit(solution)/shard_map/ppermute | solution.py:311
  88.5 0.7 collective-permute-start.3
  89.9 16.4 %all-to-all-start.2 = ((f32[8,80,128]{2,1,0:T(8,128)}), f32[8,80,128]{2,1,0:T(8,128)S(1)}, u32[]{:S(2)}, u32[]{:S(2)}) async-start(f32[8,80,128]{2,1,0:T(8,128)} %spread.1), calls=%async_computation.2 | async-start | bytes 655360 | tf_op jit(solution)/shard_map/all_to_all | solution.py:315

commit v7 on v6

--- a/solution.py
+++ b/solution.py
@@ -338,7 +338,8 @@
 
     near = jnp.sum(s_all[:, :40], axis=0)
     mirror = swap(near[:32], across)
-    own = s_all[:, 40:]
+    mirror, late = lax.optimization_barrier((mirror, s_all))
+    own = late[:, 40:]
     got = swap(own)
     rows = exchange(spread(near, mirror, g_own), ("y", "zh"))
     precond_grad = final(core, inverse_a, own, got, inv_own, inv_got)

time: 111 us -> 111 us (level); the launches traced: 109 us -> 111 us
  waiting for transfers between devices: 10.7 us -> 12 us
    all_to_all x2, waiting for transfers between devices: 6.2 us -> 7.52 us  [exchange(): return lax.all_to_all(array, axes, 0, 0, tiled=True)]
where the time goes in v7:
time: 111 us
  Pallas kernels  34.8 us (31%)
  blocking collectives  34.1 us (31%)
  starting transfers between devices  27.3 us (25%)
  waiting for transfers between devices  12 us (11%)
  local copies, waits for them, and re-layouts  1.91 us (2%)
    all_to_all x1, blocking collectives, exchange(): return lax.all_to_all(array, axes, 0, 0, tiled=True)  34.1 us
    all_to_all x2, starting transfers between devices, exchange(): return lax.all_to_all(array, axes, 0, 0, tiled=True)  20.8 us
    pallas_call x1, Pallas kernels, stat_parts(): pl.pallas_call(stat_kernel, in_specs=[in_smem(), in_hbm()], out_specs=[in...  17.3 us
    pallas_call x1, Pallas kernels, grad_parts(): pl.pallas_call(grad_kernel, in_specs=[in_smem(), in_hbm(), in_hbm()], out...  10.6 us
    all_to_all x2, waiting for transfers between devices, exchange(): return lax.all_to_all(array, axes, 0, 0, tiled=True)  7.52 us
    ppermute x5, starting transfers between devices, swap(): return lax.ppermute(array, SUB, [(i, to(i)) for i in range(128)])  6.47 us
    ppermute x5, waiting for transfers between devices, swap(): return lax.ppermute(array, SUB, [(i, to(i)) for i in range(128)])  4.48 us
    pallas_call x1, Pallas kernels, blend(): pl.pallas_call(lambda *refs: blend_kernel(*refs, total_rows=total_rows),...  2.52 us
  transfers between devices with their start and end apart: 7, of which 4 were waited for; matrix products, arithmetic and copies ran while one was open for 1% of the time, Pallas kernels for 18%

profile of v7, /device:TPU:1, one launch (start us, length us, event | category | flops | bytes accessed | tf_op | source)
XLA Modules:
  0.0 111.0 jit_solution(17245294400536034719)
XLA Ops:
  0.6 10.6 %grad_parts.1 = (f32[64,24,128]{2,1,0:T(8,128)}, f32[64,24,128]{2,1,0:T(8,128)}) custom-call(s32[1]{0:T(128)} %bitcast.1.core_ref, f32[3072,1024]{1,0:T(8,128)} %a_hbm.3, f32[3072,256]{1,0:T(8,128)} %g_hbm.1), custom_call_target="tpu_custom_call" | custom-call | flops 6039797760 | bytes 15728640 | tf_op jit(solution)/shard_map/grad_parts/pallas_call | solution.py:98
  11.3 1.5 %collective-permute-start = (f32[64,24,128]{2,1,0:T(8,128)}, f32[64,24,128]{2,1,0:T(8,128)S(1)}, u32[]{:S(2)}, u32[]{:S(2)}) collective-permute-start(f32[64,24,128]{2,1,0:T(8,128)} %get-tuple-element.21), channel_id=1, source_target_pairs={{0,8},{1,9},{2,10},{3,11},{4,12},{5,13},{6,14},{7,15},{8,0},{9,1},... | collective-permute-start | bytes 2359304 | tf_op jit(solution)/shard_map/ppermute | solution.py:311
  12.8 0.7 dynamic_slice.3.tail_ref
  13.5 1.4 %collective-permute-done.got_ref = f32[64,24,128]{2,1,0:T(8,128)S(1)} collective-permute-done((f32[64,24,128]{2,1,0:T(8,128)}, f32[64,24,128]{2,1,0:T(8,128)S(1)}, u32[]{:S(2)}, u32[]{:S(2)}) %collective-permute-start) | collective-permute-done | bytes 786464 | tf_op jit(solution)/shard_map/ppermute | solution.py:311
  14.9 1.1 %copy-done = f32[64,24,128]{2,1,0:T(8,128)S(1)} copy-done((f32[64,24,128]{2,1,0:T(8,128)S(1)}, f32[64,24,128]{2,1,0:T(8,128)}, u32[]{:S(2)}) %copy-start) | copy-done | bytes 786456
  16.0 1.6 %grad_sum.1 = f32[64,32,128]{2,1,0:T(8,128)} custom-call(f32[64,24,128]{2,1,0:T(8,128)S(1)} %copy-done, f32[64,24,128]{2,1,0:T(8,128)S(1)} %collective-permute-done.got_ref, f32[8,128]{1,0:T(8,128)S(1)} %dynamic_slice.3.tail_ref), custom_call_target="tpu_custom_call" | custom-call | tf_op jit(solution)/shard_map/grad_sum/pallas_call | solution.py:201
  17.6 11.2 %all-to-all-start = ((f32[64,32,128]{2,1,0:T(8,128)}), f32[64,32,128]{2,1,0:T(8,128)S(1)}, u32[]{:S(2)}, u32[]{:S(2)}) async-start(f32[64,32,128]{2,1,0:T(8,128)} %grad_sum.1), calls=%async_computation | async-start | bytes 2097152 | tf_op jit(solution)/shard_map/all_to_all | solution.py:315
  28.8 17.3 %stat_parts.1 = (f32[64,40,128]{2,1,0:T(8,128)S(1)}, f32[64,40,128]{2,1,0:T(8,128)}) custom-call(s32[1]{0:T(128)} %bitcast.1.core_ref, f32[3072,1024]{1,0:T(8,128)} %a_hbm.3), custom_call_target="tpu_custom_call" | custom-call | flops 12884901888 | bytes 12582912 | tf_op jit(solution)/shard_map/stat_parts/pallas_call | solution.py:171
  46.1 0.5 all-to-all-done
  46.6 2.0 %collective-permute-start.1 = (f32[64,40,128]{2,1,0:T(8,128)}, f32[64,40,128]{2,1,0:T(8,128)S(1)}, u32[]{:S(2)}, u32[]{:S(2)}) collective-permute-start(f32[64,40,128]{2,1,0:T(8,128)} %get-tuple-element.27), channel_id=1, source_target_pairs={{0,8},{1,9},{2,10},{3,11},{4,12},{5,13},{6,14},{7,15},{8,0},{9,1},... | collective-permute-start | bytes 3932168 | tf_op jit(solution)/shard_map/ppermute | solution.py:311
  48.6 0.1 collective-permute-start.2
  48.7 0.1 slice_reduce_fusion.1.tail_ref.tile_ref
  48.8 3.0 %collective-permute-done.1.got_ref = f32[64,40,128]{2,1,0:T(8,128)S(1)} collective-permute-done((f32[64,40,128]{2,1,0:T(8,128)}, f32[64,40,128]{2,1,0:T(8,128)S(1)}, u32[]{:S(2)}, u32[]{:S(2)}) %collective-permute-start.1) | collective-permute-done | bytes 1310752 | tf_op jit(solution)/shard_map/ppermute | solution.py:311
  51.8 0.2 stat_sum.1
  52.1 34.1 %all_to_all.15 = f32[64,56,128]{2,1,0:T(8,128)S(1)} all-to-all(f32[64,56,128]{2,1,0:T(8,128)S(1)} %stat_sum.1), channel_id=1, replica_groups=mesh['x'=4,'zl'=2,'co'=2,'y'=4,'zh'=2] {'x','zl','y','zh'}, dimensions={0} | all-to-all | bytes 3670016 | tf_op jit(solution)/shard_map/all_to_all | solution.py:315
  86.2 0.1 slice_reduce_fusion.near_ref
  86.3 0.0 copy-start.1
  86.3 0.8 collective-permute-start.3
  87.2 2.1 %collective-permute-start.4 = (f32[64,16,128]{2,1,0:T(8,128)S(1)}, f32[64,16,128]{2,1,0:T(8,128)S(1)}, u32[]{:S(2)}, u32[]{:S(2)}) collective-permute-start(f32[64,16,128]{2,1,0:T(8,128)S(1)} %slice.19.own_ref), channel_id=1, source_target_pairs={{0,8},{1,9},{2,10},{3,11},{4,12},{5,13},{6,14},{7,15},{8,0},{9,1},... | collective-permute-start | bytes 1572872 | tf_op jit(solution)/shard_map/ppermute | solution.py:311
  89.3 0.8 spread.1
  90.0 9.6 %all-to-all-start.2 = ((f32[8,80,128]{2,1,0:T(8,128)}), f32[8,80,128]{2,1,0:T(8,128)S(1)}, u32[]{:S(2)}, u32[]{:S(2)}) async-start(f32[8,80,128]{2,1,0:T(8,128)} %spread.1), calls=%async_computation.2 | async-start | bytes 655360 | tf_op jit(solution)/shard_map/all_to_all | solution.py:315
  99.6 1.8 %final.1 = f32[64,256]{1,0:T(8,128)} custom-call(s32[1]{0:T(128)} %bitcast.1.core_ref, f32[64,1024]{1,0:T(8,128)S(1)} %copy-done.2, f32[64,16,128]{2,1,0:T(8,128)S(1)} %slice.19.own_ref, f32[64,16,128]{2,1,0:T(8,128)S(1)} %collective-permute-done.4.got_ref, f32[64,8,128]{2,1,0:T(8,128)S(1)} %slice.16.inv_own_ref, ...), custom_call_target="tpu_custom_call" | custom-call | tf_op jit(solution)/shard_map/final/pallas_call | solution.py:290
  101.4 7.1 %all-to-all-done.2.refs_1_ = f32[8,80,128]{2,1,0:T(8,128)S(1)} async-done(((f32[8,80,128]{2,1,0:T(8,128)}), f32[8,80,128]{2,1,0:T(8,128)S(1)}, u32[]{:S(2)}, u32[]{:S(2)}) %all-to-all-start.2) | async-done | bytes 327712 | tf_op jit(solution)/shard_map/all_to_all | solution.py:315
  108.5 2.5 %blend.1 = (f32[64,1024]{1,0:T(8,128)}, f32[16,256]{1,0:T(8,128)}) custom-call(s32[1]{0:T(128)} %bitcast.refs_0_, f32[8,80,128]{2,1,0:T(8,128)S(1)} %all-to-all-done.2.refs_1_, f32[64,1024]{1,0:T(8,128)S(1)} %copy-done.1, f32[16,256]{1,0:T(8,128)S(1)} %copy-done.3), custom_call_target="tpu_custom_call" | custom-call | tf_op jit(solution)/shard_map/blend/pallas_call | solution.py:260
  (12 shorter events, 0.1 us)
Async XLA Ops:
  11.3 3.6 %collective-permute-start = (f32[64,24,128]{2,1,0:T(8,128)}, f32[64,24,128]{2,1,0:T(8,128)S(1)}, u32[]{:S(2)}, u32[]{:S(2)}) collective-permute-start(f32[64,24,128]{2,1,0:T(8,128)} %get-tuple-element.21), channel_id=1, source_target_pairs={{0,8},{1,9},{2,10},{3,11},{4,12},{5,13},{6,14},{7,15},{8,0},{9,1},... | collective-permute-start | bytes 2359304 | tf_op jit(solution)/shard_map/ppermute | solution.py:311
  14.9 1.1 %copy-start = (f32[64,24,128]{2,1,0:T(8,128)S(1)}, f32[64,24,128]{2,1,0:T(8,128)}, u32[]{:S(2)}) copy-start(f32[64,24,128]{2,1,0:T(8,128)} %get-tuple-element.20.mine_ref) | copy-start | bytes 2359300
  17.6 29.0 %all-to-all-start = ((f32[64,32,128]{2,1,0:T(8,128)}), f32[64,32,128]{2,1,0:T(8,128)S(1)}, u32[]{:S(2)}, u32[]{:S(2)}) async-start(f32[64,32,128]{2,1,0:T(8,128)} %grad_sum.1), calls=%async_computation | async-start | bytes 2097152 | tf_op jit(solution)/shard_map/all_to_all | solution.py:315
  46.6 5.2 %collective-permute-start.1 = (f32[64,40,128]{2,1,0:T(8,128)}, f32[64,40,128]{2,1,0:T(8,128)S(1)}, u32[]{:S(2)}, u32[]{:S(2)}) collective-permute-start(f32[64,40,128]{2,1,0:T(8,128)} %get-tuple-element.27), channel_id=1, source_target_pairs={{0,8},{1,9},{2,10},{3,11},{4,12},{5,13},{6,14},{7,15},{8,0},{9,1},... | collective-permute-start | bytes 3932168 | tf_op jit(solution)/shard_map/ppermute | solution.py:311
  48.6 3.4 %collective-permute-start.2 = (f32[64,8,128]{2,1,0:T(8,128)S(1)}, f32[64,8,128]{2,1,0:T(8,128)S(1)}, u32[]{:S(2)}, u32[]{:S(2)}) collective-permute-start(f32[64,8,128]{2,1,0:T(8,128)S(1)} %slice.16.inv_own_ref), channel_id=1, source_target_pairs={{0,8},{1,9},{2,10},{3,11},{4,12},{5,13},{6,14},{7,15},{8,0},{9,1},... | collective-permute-start | bytes 786440 | tf_op jit(solution)/shard_map/ppermute | solution.py:311
  86.2 13.4 %copy-start.2 = (f32[64,1024]{1,0:T(8,128)S(1)}, f32[64,1024]{1,0:T(8,128)}, u32[]{:S(2)}) copy-start(f32[64,1024]{1,0:T(8,128)} %inv_a_ref.1) | copy-start | bytes 786436
  86.3 22.2 %copy-start.1 = (f32[64,1024]{1,0:T(8,128)S(1)}, f32[64,1024]{1,0:T(8,128)}, u32[]{:S(2)}) copy-start(f32[64,1024]{1,0:T(8,128)} %refs_2_.1) | copy-start | bytes 786436
  86.3 22.1 %copy-start.3 = (f32[16,256]{1,0:T(8,128)S(1)}, f32[16,256]{1,0:T(8,128)}, u32[]{:S(2)}) copy-start(f32[16,256]{1,0:T(8,128)} %refs_3_.1) | copy-start | bytes 49156
  86.3 0.8 collective-permute-start.3
  87.2 12.4 %collective-permute-start.4 = (f32[64,16,128]{2,1,0:T(8,128)S(1)}, f32[64,16,128]{2,1,0:T(8,128)S(1)}, u32[]{:S(2)}, u32[]{:S(2)}) collective-permute-start(f32[64,16,128]{2,1,0:T(8,128)S(1)} %slice.19.own_ref), channel_id=1, source_target_pairs={{0,8},{1,9},{2,10},{3,11},{4,12},{5,13},{6,14},{7,15},{8,0},{9,1},... | collective-permute-start | bytes 1572872 | tf_op jit(solution)/shard_map/ppermute | solution.py:311
  90.0 18.4 %all-to-all-start.2 = ((f32[8,80,128]{2,1,0:T(8,128)}), f32[8,80,128]{2,1,0:T(8,128)S(1)}, u32[]{:S(2)}, u32[]{:S(2)}) async-start(f32[8,80,128]{2,1,0:T(8,128)} %spread.1), calls=%async_computation.2 | async-start | bytes 655360 | tf_op jit(solution)/shard_map/all_to_all | solution.py:315
